TPU v7x, 128 devices: a whole 4x4x4 slice. The times are simulated.
128 devices in a mesh: seq: 32 (over x, z, core), rows: 4 (over y).
Axes of the slice: x: 4, y: 4, z: 4, core: 2. Of those that a mesh axis runs over, the one named last changes fastest.
Arguments:
- tokens: bfloat16 [8, 2048, 2048], P('rows', 'seq'), may hold values from -6 to 6
- seg_starts: int32 [8, 4], P('rows'), may hold values from 0 to 2048, as said below
- gain_one: bfloat16 [2048], P(('seq', 'rows')), may hold values from 0.5 to 1.5
- gain_two: bfloat16 [2048], P(('seq', 'rows')), may hold values from 0.5 to 1.5
- conv_weight: bfloat16 [4, 2560], P(None, ('seq', 'rows')), may hold values from -3 to 3
- conv_bias: bfloat16 [2560], P(('seq', 'rows')), may hold values from -3 to 3
- rate_weight: bfloat16 [2560, 160], P(('seq', 'rows')), may hold values from -0.5 to 0.5
- input_weight: bfloat16 [2560, 160], P(('seq', 'rows')), may hold values from -0.5 to 0.5
- rate_bias: bfloat16 [2560], P(('seq', 'rows')), may hold values from -4 to 4
- input_bias: bfloat16 [2560], P(('seq', 'rows')), may hold values from -4 to 4
- decay_param: bfloat16 [2560], P(('seq', 'rows')), may hold values from 4 to 12
- proj_out: bfloat16 [2048, 2560], P(('seq', 'rows')), may hold values from -0.125 to 0.125
- proj_x: bfloat16 [2048, 2560], P(('seq', 'rows')), may hold values from -0.125 to 0.125
- proj_y: bfloat16 [2048, 2560], P(('seq', 'rows')), may hold values from -0.125 to 0.125
- ffn_gate: bfloat16 [2048, 6144], P(('seq', 'rows')), may hold values from -0.125 to 0.125
- ffn_up: bfloat16 [2048, 6144], P(('seq', 'rows')), may hold values from -0.125 to 0.125
- ffn_down: bfloat16 [2048, 6144], P(('seq', 'rows')), may hold values from -0.078125 to 0.078125
- cotangent: bfloat16 [8, 2048, 2048], P('rows', 'seq'), may hold values from -6 to 6
Outputs:
- output: bfloat16 [8, 2048, 2048], P('rows', 'seq')
- grad_tokens: bfloat16 [8, 2048, 2048], P('rows', 'seq')
- grad_gain_one: float32 [2048], P(('seq', 'rows'))
- grad_gain_two: float32 [2048], P(('seq', 'rows'))
- grad_conv_weight: float32 [4, 2560], P(None, ('seq', 'rows'))
- grad_conv_bias: float32 [2560], P(('seq', 'rows'))
- grad_rate_weight: float32 [2560, 160], P(('seq', 'rows'))
- grad_input_weight: float32 [2560, 160], P(('seq', 'rows'))
- grad_rate_bias: float32 [2560], P(('seq', 'rows'))
- grad_input_bias: float32 [2560], P(('seq', 'rows'))
- grad_decay_param: float32 [2560], P(('seq', 'rows'))
- grad_proj_out: float32 [2048, 2560], P(('seq', 'rows'))
- grad_proj_x: float32 [2048, 2560], P(('seq', 'rows'))
- grad_proj_y: float32 [2048, 2560], P(('seq', 'rows'))
- grad_ffn_gate: float32 [2048, 6144], P(('seq', 'rows'))
- grad_ffn_up: float32 [2048, 6144], P(('seq', 'rows'))
- grad_ffn_down: float32 [2048, 6144], P(('seq', 'rows'))
Inputs may be any that keep to these rules, and one draw needn't show every extreme that they name: `seg_starts`: in each row the entries rise and the first is 0; an entry equal to 2048 marks no document. In every aligned group of 2 rows exactly one row holds a single document over the whole row; the other rows hold 4 documents.
All inputs are finite; a program needn't handle non-finite values.
Results may differ from a plain program's by a relative error of at most 0.017.
Values may be sent and summed in bfloat16 or wider, within the bound.
A program may use at most 256 MiB of HBM per device.

v0:
```python
import jax
import jax.numpy as jnp
from jax import lax
from jax.sharding import PartitionSpec as P

EPSILON = 1e-06
FLOOR_VALUE = 0.001


def from_behind(block, axis, distance):
    devices = range(lax.axis_size(axis))
    route = [(i - distance, i) for i in devices if i - distance in devices]
    return lax.ppermute(block, axis, route)


def prefix(value, axis, combine, identity, reverse):
    devices, position = (lax.axis_size(axis), lax.axis_index(axis))
    everything = jax.tree.map(lambda part: lax.all_gather(part, axis), value)
    start = jax.tree.map(
        lambda part, zero: jnp.broadcast_to(jnp.asarray(zero, part.dtype), part.shape),
        value,
        identity,
    )

    def lap(k, before):
        at = devices - 1 - k if reverse else k
        reached = at > position if reverse else at < position
        new = combine(before, jax.tree.map(lambda part: part[at], everything))
        return jax.tree.map(lambda a, b: jnp.where(reached, a, b), new, before)

    return lax.fori_loop(0, devices, lap, start)


def rms_norm(values):
    return values * lax.rsqrt(jnp.mean(values * values, axis=-1, keepdims=True) + EPSILON)


def gelu_tanh(values):
    return jax.nn.gelu(values, approximate=True)


def gated_product(gate_pre, up_pre):
    return gelu_tanh(gate_pre) * up_pre


def combine(earlier, latter):
    return (earlier[0] * latter[0], latter[0] * earlier[1] + latter[1])


def decay_terms(conv_out, rate_pre, input_pre, rate_bias, input_bias, decay_param, resets):
    rate_gate = jax.nn.sigmoid(rate_pre + rate_bias)
    input_gate = jax.nn.sigmoid(input_pre + input_bias)
    log_decay = -8.0 * rate_gate * jax.nn.softplus(-decay_param)
    keep_mask = 1.0 - resets
    factor = jnp.exp(log_decay) * keep_mask
    scale_term = jnp.where(
        resets > 0.5, 1.0, jnp.sqrt(jnp.maximum(-jnp.expm1(2.0 * log_decay), FLOOR_VALUE))
    )
    return (factor, scale_term * (input_gate * conv_out))


def contract_last(left, right):
    return lax.dot_general(
        left, right, (((1,), (1,)), ((), ())), preferred_element_type=jnp.float32
    )


def contract_first(left, right):
    return lax.dot_general(
        left, right, (((0,), (0,)), ((), ())), preferred_element_type=jnp.float32
    )


def local(
    tokens,
    seg_starts,
    gain_one,
    gain_two,
    conv_weight,
    conv_bias,
    rate_weight,
    input_weight,
    rate_bias,
    input_bias,
    decay_param,
    proj_out,
    proj_x,
    proj_y,
    ffn_gate,
    ffn_up,
    ffn_down,
    cotangent,
):
    slot_count, span_len, model_width = tokens.shape
    total_rows = slot_count * span_len
    tap_count = conv_weight.shape[0]
    head_size = rate_weight.shape[1]
    gathered = (
        lax.all_gather(gain_one, ("seq", "rows"), axis=0, tiled=True),
        lax.all_gather(gain_two, ("seq", "rows"), axis=0, tiled=True),
        lax.all_gather(conv_weight, ("seq", "rows"), axis=1, tiled=True),
        lax.all_gather(conv_bias, ("seq", "rows"), axis=0, tiled=True),
        lax.all_gather(rate_weight, ("seq", "rows"), axis=0, tiled=True),
        lax.all_gather(input_weight, ("seq", "rows"), axis=0, tiled=True),
        lax.all_gather(rate_bias, ("seq", "rows"), axis=0, tiled=True),
        lax.all_gather(input_bias, ("seq", "rows"), axis=0, tiled=True),
        lax.all_gather(decay_param, ("seq", "rows"), axis=0, tiled=True),
        lax.all_gather(proj_out, ("seq", "rows"), axis=0, tiled=True),
    )
    gain_a = gathered[0].astype(jnp.float32)
    gain_b = gathered[1].astype(jnp.float32)
    conv_full = gathered[2].astype(jnp.float32)
    conv_shift = gathered[3].astype(jnp.float32)
    rate_blocks = gathered[4].reshape(-1, head_size, head_size)
    input_blocks = gathered[5].reshape(-1, head_size, head_size)
    rate_shift = gathered[6].astype(jnp.float32)
    input_shift = gathered[7].astype(jnp.float32)
    decay_full = gathered[8].astype(jnp.float32)
    out_full = gathered[9]
    lru_width = out_full.shape[1]
    first_pos = lax.axis_index("seq") * span_len
    positions = first_pos + jnp.arange(span_len, dtype=jnp.int32)

    def doc_number(where):
        return jnp.sum((seg_starts[:, None, :] <= where[None, :, None]).astype(jnp.int32), axis=2)

    current = doc_number(positions)
    resets = jnp.any(seg_starts[:, None, :] == positions[None, :, None], axis=2).astype(
        jnp.float32
    )[:, :, None]
    validity = []
    for tap_index in range(tap_count):
        behind = positions - tap_index
        usable = (behind >= 0)[None, :] & (doc_number(behind) == current)
        validity.append(usable.astype(jnp.float32)[:, :, None])
    flat_tokens = tokens.reshape(total_rows, model_width).astype(jnp.float32)
    normed_one = rms_norm(flat_tokens)
    scaled_one = (normed_one * gain_a).astype(jnp.bfloat16)
    whole_x, whole_y = (
        lax.all_gather(proj_x, ("seq", "rows"), axis=0, tiled=True),
        lax.all_gather(proj_y, ("seq", "rows"), axis=0, tiled=True),
    )
    pre_x = jnp.dot(scaled_one, whole_x, preferred_element_type=jnp.float32)
    pre_flat_y = jnp.dot(scaled_one, whole_y, preferred_element_type=jnp.float32)
    conv_in = pre_x.astype(jnp.bfloat16).reshape(slot_count, span_len, lru_width)
    rim_rows = from_behind(conv_in[:, span_len - (tap_count - 1) :, :], "seq", 1)
    extended = jnp.concatenate([rim_rows, conv_in], axis=1).astype(jnp.float32)
    conv_out = conv_shift
    for tap_index in range(tap_count):
        offset = tap_count - 1 - tap_index
        conv_out = (
            conv_out
            + conv_full[tap_index] * validity[tap_index] * extended[:, offset : offset + span_len]
        )
    conv_low = conv_out.astype(jnp.bfloat16).reshape(total_rows, -1, head_size)
    rate_pre = jnp.einsum(
        "thi,hij->thj", conv_low, rate_blocks, preferred_element_type=jnp.float32
    ).reshape(slot_count, span_len, lru_width)
    input_pre = jnp.einsum(
        "thi,hij->thj", conv_low, input_blocks, preferred_element_type=jnp.float32
    ).reshape(slot_count, span_len, lru_width)
    factor, drive_term = decay_terms(
        conv_out, rate_pre, input_pre, rate_shift, input_shift, decay_full, resets
    )
    decay_prod, local_states = lax.associative_scan(combine, (factor, drive_term), axis=1)
    unit_init = jnp.ones((slot_count, lru_width), jnp.float32)
    zero_state = jnp.zeros((slot_count, lru_width), jnp.float32)
    carried = prefix(
        (decay_prod[:, -1], local_states[:, -1]), "seq", combine, (unit_init, zero_state), False
    )[1]
    states = local_states + decay_prod * carried[:, None, :]
    pre_y = pre_flat_y.reshape(slot_count, span_len, lru_width)
    gate_y = gelu_tanh(pre_y)
    mixed_low = (states * gate_y).astype(jnp.bfloat16).reshape(total_rows, lru_width)
    residual = flat_tokens + contract_last(mixed_low, out_full)
    normed_two = rms_norm(residual)
    scaled_two = (normed_two * gain_b).astype(jnp.bfloat16)
    cot_low = cotangent.reshape(total_rows, model_width)
    grad_out = cot_low.astype(jnp.float32)
    gate_cols, up_cols, down_cols = (
        lax.all_to_all(ffn_gate, "rows", split_axis=1, concat_axis=0, tiled=True),
        lax.all_to_all(ffn_up, "rows", split_axis=1, concat_axis=0, tiled=True),
        lax.all_to_all(ffn_down, "rows", split_axis=1, concat_axis=0, tiled=True),
    )
    gate_cols, up_cols, down_cols = (
        lax.all_gather(gate_cols, "seq", axis=0, tiled=True),
        lax.all_gather(up_cols, "seq", axis=0, tiled=True),
        lax.all_gather(down_cols, "seq", axis=0, tiled=True),
    )
    group_rows, group_cot = (
        lax.all_gather(scaled_two, "rows", axis=0, tiled=True),
        lax.all_gather(cot_low, "rows", axis=0, tiled=True),
    )
    gate_pre = jnp.dot(group_rows, gate_cols, preferred_element_type=jnp.float32)
    up_pre = jnp.dot(group_rows, up_cols, preferred_element_type=jnp.float32)
    hidden_low = gated_product(gate_pre, up_pre).astype(jnp.bfloat16)
    ffn_result = lax.psum_scatter(
        contract_last(hidden_low, down_cols).astype(jnp.bfloat16),
        "rows",
        scatter_dimension=0,
        tiled=True,
    ).astype(jnp.float32)
    output = (residual + ffn_result).astype(jnp.bfloat16).reshape(tokens.shape)
    grad_hidden = jnp.dot(group_cot, down_cols, preferred_element_type=jnp.float32)
    grad_down = contract_first(group_cot, hidden_low)
    _, gated_pull = jax.vjp(gated_product, gate_pre, up_pre)
    grad_gate_pre, grad_up_pre = gated_pull(grad_hidden)
    grad_gate_low = grad_gate_pre.astype(jnp.bfloat16)
    grad_up_low = grad_up_pre.astype(jnp.bfloat16)
    grad_gate_w = contract_first(group_rows, grad_gate_low)
    grad_up_w = contract_first(group_rows, grad_up_low)
    grad_scaled_two = lax.psum_scatter(
        (contract_last(grad_gate_low, gate_cols) + contract_last(grad_up_low, up_cols)).astype(
            jnp.bfloat16
        ),
        "rows",
        scatter_dimension=0,
        tiled=True,
    ).astype(jnp.float32)
    column_sums = (
        lax.psum_scatter(
            grad_gate_w.astype(jnp.bfloat16), "seq", scatter_dimension=0, tiled=True
        ).astype(jnp.float32),
        lax.psum_scatter(
            grad_up_w.astype(jnp.bfloat16), "seq", scatter_dimension=0, tiled=True
        ).astype(jnp.float32),
        lax.psum_scatter(
            grad_down.astype(jnp.bfloat16), "seq", scatter_dimension=0, tiled=True
        ).astype(jnp.float32),
    )
    ffn_sums = (
        lax.all_to_all(
            column_sums[0].astype(jnp.bfloat16), "rows", split_axis=0, concat_axis=1, tiled=True
        ).astype(jnp.float32),
        lax.all_to_all(
            column_sums[1].astype(jnp.bfloat16), "rows", split_axis=0, concat_axis=1, tiled=True
        ).astype(jnp.float32),
        lax.all_to_all(
            column_sums[2].astype(jnp.bfloat16), "rows", split_axis=0, concat_axis=1, tiled=True
        ).astype(jnp.float32),
    )
    grad_gain_b = jnp.sum(grad_scaled_two * normed_two, axis=0)
    _, second_pull = jax.vjp(rms_norm, residual)
    grad_residual = grad_out + second_pull(grad_scaled_two * gain_b)[0]
    branch_grad_low = grad_residual.astype(jnp.bfloat16)
    grad_mixed = jnp.dot(branch_grad_low, out_full, preferred_element_type=jnp.float32).reshape(
        slot_count, span_len, lru_width
    )
    grad_proj_out = contract_first(branch_grad_low, mixed_low)
    grad_states = grad_mixed * gate_y
    _, gelu_pull = jax.vjp(gelu_tanh, pre_y)
    grad_y_low = (
        gelu_pull(grad_mixed * states)[0].astype(jnp.bfloat16).reshape(total_rows, lru_width)
    )
    next_factor = jnp.concatenate([factor[:, 1:], jnp.ones_like(factor[:, :1])], axis=1)
    later_prod, local_adjoint = lax.associative_scan(
        combine, (next_factor, grad_states), reverse=True, axis=1
    )
    incoming = prefix(
        (decay_prod[:, -1], factor[:, 0] * local_adjoint[:, 0]),
        "seq",
        combine,
        (unit_init, zero_state),
        True,
    )[1]
    adjoint = local_adjoint + later_prod * incoming[:, None, :]
    previous = jnp.concatenate([carried[:, None, :], states[:, :-1]], axis=1)

    def gate_terms(
        conv_values, rate_values, input_values, rate_bias_full, input_bias_full, decay_values
    ):
        return decay_terms(
            conv_values,
            rate_values,
            input_values,
            rate_bias_full,
            input_bias_full,
            decay_values,
            resets,
        )

    _, gate_pull = jax.vjp(
        gate_terms, conv_out, rate_pre, input_pre, rate_shift, input_shift, decay_full
    )
    grad_conv_direct, grad_rate_pre, grad_input_pre, grad_rate_bias, grad_input_bias, grad_decay = (
        gate_pull((adjoint * previous, adjoint))
    )
    grad_rate_low = grad_rate_pre.astype(jnp.bfloat16).reshape(total_rows, -1, head_size)
    grad_input_low = grad_input_pre.astype(jnp.bfloat16).reshape(total_rows, -1, head_size)
    grad_rate_w = jnp.einsum(
        "thi,thj->hij", conv_low, grad_rate_low, preferred_element_type=jnp.float32
    ).reshape(lru_width, head_size)
    grad_input_w = jnp.einsum(
        "thi,thj->hij", conv_low, grad_input_low, preferred_element_type=jnp.float32
    ).reshape(lru_width, head_size)
    grad_from_gates = jnp.einsum(
        "thj,hij->thi", grad_rate_low, rate_blocks, preferred_element_type=jnp.float32
    ) + jnp.einsum("thj,hij->thi", grad_input_low, input_blocks, preferred_element_type=jnp.float32)
    grad_conv = grad_conv_direct + grad_from_gates.reshape(slot_count, span_len, lru_width)
    grad_extended = jnp.zeros((slot_count, span_len + tap_count - 1, lru_width), jnp.float32)
    conv_grad_rows = []
    for tap_index in range(tap_count):
        offset = tap_count - 1 - tap_index
        weighted = grad_conv * validity[tap_index]
        conv_grad_rows.append(
            jnp.sum(weighted * extended[:, offset : offset + span_len], axis=(0, 1))
        )
        grad_extended = grad_extended + jnp.pad(
            conv_full[tap_index] * weighted, ((0, 0), (offset, tap_count - 1 - offset), (0, 0))
        )
    grad_conv_w = jnp.stack(conv_grad_rows, axis=0)
    grad_conv_b = jnp.sum(grad_conv, axis=(0, 1))
    rim_grad = from_behind(
        grad_extended[:, : tap_count - 1].astype(jnp.bfloat16), "seq", -1
    ).astype(jnp.float32)
    grad_conv_in = grad_extended[:, tap_count - 1 :] + jnp.pad(
        rim_grad, ((0, 0), (span_len - (tap_count - 1), 0), (0, 0))
    )
    grad_x_low = grad_conv_in.astype(jnp.bfloat16).reshape(total_rows, lru_width)
    grad_proj_x = contract_first(scaled_one, grad_x_low)
    grad_proj_y = contract_first(scaled_one, grad_y_low)
    grad_scaled_one = contract_last(grad_x_low, whole_x) + contract_last(grad_y_low, whole_y)
    grad_gain_a = jnp.sum(grad_scaled_one * normed_one, axis=0)
    _, first_pull = jax.vjp(rms_norm, flat_tokens)
    grad_tokens = (
        (grad_residual + first_pull(grad_scaled_one * gain_a)[0])
        .astype(jnp.bfloat16)
        .reshape(tokens.shape)
    )
    mixer_sums = (
        lax.psum_scatter(grad_gain_a, ("seq", "rows"), scatter_dimension=0, tiled=True),
        lax.psum_scatter(grad_gain_b, ("seq", "rows"), scatter_dimension=0, tiled=True),
        lax.psum_scatter(grad_conv_w, ("seq", "rows"), scatter_dimension=1, tiled=True),
        lax.psum_scatter(grad_conv_b, ("seq", "rows"), scatter_dimension=0, tiled=True),
        lax.psum_scatter(grad_rate_w, ("seq", "rows"), scatter_dimension=0, tiled=True),
        lax.psum_scatter(grad_input_w, ("seq", "rows"), scatter_dimension=0, tiled=True),
        lax.psum_scatter(grad_rate_bias, ("seq", "rows"), scatter_dimension=0, tiled=True),
        lax.psum_scatter(grad_input_bias, ("seq", "rows"), scatter_dimension=0, tiled=True),
        lax.psum_scatter(grad_decay, ("seq", "rows"), scatter_dimension=0, tiled=True),
        lax.psum_scatter(grad_proj_out, ("seq", "rows"), scatter_dimension=0, tiled=True),
        lax.psum_scatter(grad_proj_x, ("seq", "rows"), scatter_dimension=0, tiled=True),
        lax.psum_scatter(grad_proj_y, ("seq", "rows"), scatter_dimension=0, tiled=True),
    )
    return (
        output,
        grad_tokens,
        mixer_sums[0],
        mixer_sums[1],
        mixer_sums[2],
        mixer_sums[3],
        mixer_sums[4],
        mixer_sums[5],
        mixer_sums[6],
        mixer_sums[7],
        mixer_sums[8],
        mixer_sums[9],
        mixer_sums[10],
        mixer_sums[11],
        ffn_sums[0],
        ffn_sums[1],
        ffn_sums[2],
    )


def solution(mesh):
    return jax.shard_map(
        local,
        mesh=mesh,
        in_specs=(
            P("rows", "seq", None),
            P("rows", None),
            P(("seq", "rows")),
            P(("seq", "rows")),
            P(None, ("seq", "rows")),
            P(("seq", "rows")),
            P(("seq", "rows"), None),
            P(("seq", "rows"), None),
            P(("seq", "rows")),
            P(("seq", "rows")),
            P(("seq", "rows")),
            P(("seq", "rows"), None),
            P(("seq", "rows"), None),
            P(("seq", "rows"), None),
            P(("seq", "rows"), None),
            P(("seq", "rows"), None),
            P(("seq", "rows"), None),
            P("rows", "seq", None),
        ),
        out_specs=(
            P("rows", "seq", None),
            P("rows", "seq", None),
            P(("seq", "rows")),
            P(("seq", "rows")),
            P(None, ("seq", "rows")),
            P(("seq", "rows")),
            P(("seq", "rows"), None),
            P(("seq", "rows"), None),
            P(("seq", "rows")),
            P(("seq", "rows")),
            P(("seq", "rows")),
            P(("seq", "rows"), None),
            P(("seq", "rows"), None),
            P(("seq", "rows"), None),
            P(("seq", "rows"), None),
            P(("seq", "rows"), None),
            P(("seq", "rows"), None),
        ),
        check_vma=False,
    )
```

profile of v0, /device:TPU:0, one launch (start us, length us, event | category | flops | bytes accessed | tf_op | source)
XLA Modules:
  0.0 3488.1 jit_solution(3482523068212462280)
XLA Ops:
  11.1 4.5 all-to-all-start
  20.7 69.0 %all-reduce.73 = (bf16[2560]{0:T(1024)(128)(2,1)S(1)}, bf16[2048]{0:T(1024)(128)(2,1)S(1)}, bf16[2560]{0:T(1024)(128)(2,1)S(1)}, bf16[2560]{0:T(1024)(128)(2,1)S...) all-reduce(bf16[2560]{0:T(1024)(128)(2,1)S(1)} %dynamic-update-slic, ...), channel_id=1, replica_groups=mesh['seq'=32,'rows'=4] {'seq','rows'}, use_global_device_ids=true, to_apply=%add.58 | all-reduce | flops 14336 | bytes 57344
  91.1 55.8 %all-gather.3 = bf16[128,20,4]{1,2,0:T(4,128)(2,1)S(1)} all-gather(bf16[1,20,4]{1,2,0:T(4,128)(2,1)S(1)} %bitcast.226), channel_id=1, replica_groups=mesh['seq'=32,'rows'=4] {'seq','rows'}, dimensions={0}, use_global_device_ids=true | all-gather | bytes 20640 | tf_op jit(solution)/shard_map/all_gather | solution.py:101
  148.4 72.8 %all-gather.5 = bf16[128,20,160]{2,1,0:T(8,128)(2,1)} all-gather(bf16[1,20,160]{2,1,0:T(8,128)(2,1)S(1)} %bitcast.224), channel_id=1, replica_groups=mesh['seq'=32,'rows'=4] {'seq','rows'}, dimensions={0}, use_global_device_ids=true | all-gather | bytes 825600 | tf_op jit(solution)/shard_map/all_gather | solution.py:104
  221.2 70.5 %all-gather.4 = bf16[128,20,160]{2,1,0:T(8,128)(2,1)} all-gather(bf16[1,20,160]{2,1,0:T(8,128)(2,1)S(1)} %bitcast.225), channel_id=1, replica_groups=mesh['seq'=32,'rows'=4] {'seq','rows'}, dimensions={0}, use_global_device_ids=true | all-gather | bytes 825600 | tf_op jit(solution)/shard_map/all_gather | solution.py:103
  292.0 5.5 convolution_convert_fusion.3
  301.9 3.9 reshape.336
  329.5 4.4 fusion.45
  462.5 27.8 all-gather.1
  505.7 25.4 all-gather
  536.9 25.5 while.30
  562.5 9.3 multiply_convert_fusion.2
  571.7 8.7 multiply_reduce_fusion.5
  583.6 9.8 all_to_all.96
  595.2 11.9 all_to_all.97
  607.3 5.8 all-gather.21.cloned.1.call-done
  613.1 8.5 fusion.93
  621.6 42.9 %all-gather.25.cloned.1.call-done = bf16[2048,1536]{1,0:T(8,128)(2,1)} async-done(((bf16[64,1536]{1,0:T(8,128)(2,1)}), bf16[2048,1536]{1,0:T(8,128)(2,1)}) %all-gather.25.cloned.1.call-update) | async-done | bytes 6291472 | tf_op jit(solution)/shard_map/all_gather | solution.py:187
  664.5 8.5 fusion.94
  673.1 22.9 all-gather.29.cloned.1.call-done
  696.0 51.5 %all-gather.27.cloned.1.call-done = bf16[2048,1536]{1,0:T(8,128)(2,1)} async-done(((bf16[64,1536]{1,0:T(8,128)(2,1)}), bf16[2048,1536]{1,0:T(8,128)(2,1)}) %all-gather.27.cloned.1.call-update) | async-done | bytes 6291472 | tf_op jit(solution)/shard_map/all_gather | solution.py:188
  747.5 11.8 multiply_convert_fusion
  759.3 6.7 fusion.95
  766.0 4.7 add_convert_fusion
  770.8 8.0 convolution_convert_fusion.4
  792.2 9.9 slice.488
  802.1 9.9 slice.495
  811.9 9.9 slice.486
  821.8 8.2 convolution_convert_fusion.2
  835.7 5.9 fusion.56
  850.7 9.9 slice.490
  860.6 9.9 slice.492
  973.4 9.9 slice.532
  991.6 26.3 all-gather.2
  1018.0 3.5 reduce.7
  1023.8 26.0 while.31
  1066.2 10.7 rev.9
  1076.9 10.7 rev.8
  1087.7 6.4 fusion.78
  1114.8 3.8 reshape.346
  1118.7 3.7 multiply_reduce_fusion.4
  1130.8 5.2 fusion.39
  1136.1 8.1 convolution_convert_fusion.1
  1144.5 8.2 fusion.6
  1152.7 8.7 copy.157
  1162.8 8.6 fusion.54
  1172.5 8.7 convolution_bitcast_fusion
  1181.3 8.8 convolution_bitcast_fusion.1
  1195.4 361.0 %fusion.81 = (f32[24,160]{1,0:T(8,128)S(1)}, f32[24,160]{1,0:T(8,128)S(1)}) fusion(f32[2560,160]{1,0:T(8,128)} %bitcast.178, f32[2560,160]{1,0:T(8,128)} %bitcast.177), kind=kCustom, calls=%all-reduce-scatter.2 | all-reduce-scatter fusion | flops 983041 | bytes 3307520
  1566.8 9.9 collective-permute-start.30
  1584.7 7.8 collective-permute-start.35
  1592.5 11.8 collective-permute-start.36
  1604.3 4.2 collective-permute-start.37
  1608.5 5.8 collective-permute-start.38
  1658.1 4.1 collective-permute-start.3
  1671.0 4.0 collective-permute-start.8
  1677.4 30.9 concatenate.93
  1708.3 31.0 concatenate.92
  1756.3 4.8 all-to-all-start.4
  1761.2 7.0 all-to-all-done.4
  1773.1 5.6 all-to-all-done.5
  1779.5 358.2 %reduce-scatter.20.cloned.1.call-done = f32[16,2560]{1,0:T(8,128)} async-done(((f32[2048,2560]{1,0:T(8,128)}), f32[16,2560]{1,0:T(8,128)}) %reduce-scatter.20.cloned.1.call-update) | async-done | bytes 163856 | tf_op jit(solution)/shard_map/reduce_scatter | solution.py:340
  2137.7 671.5 %reduce-scatter.24.cloned.1.call-done = f32[16,2560]{1,0:T(8,128)} async-done(((f32[2048,2560]{1,0:T(8,128)}), f32[16,2560]{1,0:T(8,128)}) %reduce-scatter.24.cloned.1.call-update) | async-done | bytes 163856 | tf_op jit(solution)/shard_map/reduce_scatter | solution.py:342
  2809.2 671.9 %reduce-scatter.22.cloned.1.call-done = f32[16,2560]{1,0:T(8,128)} async-done(((f32[2048,2560]{1,0:T(8,128)}), f32[16,2560]{1,0:T(8,128)}) %reduce-scatter.22.cloned.1.call-update) | async-done | bytes 163856 | tf_op jit(solution)/shard_map/reduce_scatter | solution.py:341
  (708 shorter events, 534.9 us)
Async XLA Ops:
  7.2 284.7 %all-gather.15.cloned.1.call-start = ((), (), s32[]{:S(2)}) async-start(), calls=%async_computation.14 | async-start | bytes 10567680 | tf_op jit(solution)/shard_map/all_gather | solution.py:140
  8.0 554.5 %all-gather.17.cloned.1.call-start = ((), (), s32[]{:S(2)}) async-start(), calls=%async_computation.15 | async-start | bytes 10567680 | tf_op jit(solution)/shard_map/all_gather | solution.py:141
  8.7 563.0 %all-gather.19.cloned.1.call-start = ((), (), s32[]{:S(2)}) async-start(), calls=%async_computation.16 | async-start | bytes 10567680 | tf_op jit(solution)/shard_map/all_gather | solution.py:108
  11.1 294.8 %all-to-all-start = ((bf16[16,4,1536]{2,0,1:T(8,128)(2,1)}), bf16[16,4,1536]{2,0,1:T(8,128)(2,1)S(1)}, u32[]{:S(2)}, u32[]{:S(2)}) async-start(bf16[16,4,1536]{2,0,1:T(8,128)(2,1)} %bitcast.149), calls=%async_computation | async-start | bytes 393216 | tf_op jit(solution)/shard_map/all_to_all | solution.py:181
  15.6 591.7 %all-gather.23.cloned.1.call-start = ((), (), s32[]{:S(2)}) async-start(), calls=%async_computation.18 | async-start | bytes 6488064 | tf_op jit(solution)/shard_map/all_gather | solution.py:186
  297.5 9.1 collective-permute-start
  306.6 306.6 %all-gather.21.cloned.1.call-start = ((), (), s32[]{:S(2)}) async-start(), calls=%async_computation.17 | async-start | bytes 2621440 | tf_op jit(solution)/shard_map/all_gather | solution.py:191
  582.6 81.9 %all-gather.25.cloned.1.call-start = ((), (), s32[]{:S(2)}) async-start(), calls=%async_computation.19 | async-start | bytes 6488064 | tf_op jit(solution)/shard_map/all_gather | solution.py:187
  593.4 102.5 %all-gather.29.cloned.1.call-start = ((), (), s32[]{:S(2)}) async-start(), calls=%async_computation.22 | async-start | bytes 2621440 | tf_op jit(solution)/shard_map/all_gather | solution.py:192
  594.2 153.3 %all-gather.27.cloned.1.call-start = ((), (), s32[]{:S(2)}) async-start(), calls=%async_computation.20 | async-start | bytes 6488064 | tf_op jit(solution)/shard_map/all_gather | solution.py:188
  607.1 223.4 %reduce-scatter.18.cloned.1.call-start = ((), (), s32[]{:S(2)}) async-start(), calls=%async_computation.23 | async-start | bytes 2621440 | tf_op jit(solution)/shard_map/reduce_scatter | solution.py:212
  770.8 62.0 %reduce-scatter.16.cloned.1.call-start = ((), (), s32[]{:S(2)}) async-start(), calls=%async_computation.21 | async-start | bytes 2621440 | tf_op jit(solution)/shard_map/reduce_scatter | solution.py:197
  778.9 963.9 %reduce-scatter.26.cloned.1.call-start = ((), (), s32[]{:S(2)}) async-start(), calls=%async_computation.27 | async-start | bytes 6488064 | tf_op jit(solution)/shard_map/reduce_scatter | solution.py:221
  830.0 917.4 %all-reduce.77.cloned.1.call-start = ((), (), s32[]{:S(2)}) async-start(), calls=%async_computation.30 | async-start | bytes 212992
  1136.0 620.3 %reduce-scatter.28.cloned.1.call-start = ((), (), s32[]{:S(2)}) async-start(), calls=%async_computation.28 | async-start | bytes 6488064 | tf_op jit(solution)/shard_map/reduce_scatter | solution.py:224
  1144.2 616.9 %reduce-scatter.30.cloned.1.call-start = ((), (), s32[]{:S(2)}) async-start(), calls=%async_computation.29 | async-start | bytes 6488064 | tf_op jit(solution)/shard_map/reduce_scatter | solution.py:227
  1161.4 976.3 %reduce-scatter.20.cloned.1.call-start = ((), (), s32[]{:S(2)}) async-start(), calls=%async_computation.24 | async-start | bytes 21135360 | tf_op jit(solution)/shard_map/reduce_scatter | solution.py:340
  1171.4 1637.7 %reduce-scatter.24.cloned.1.call-start = ((), (), s32[]{:S(2)}) async-start(), calls=%async_computation.26 | async-start | bytes 21135360 | tf_op jit(solution)/shard_map/reduce_scatter | solution.py:342
  1181.2 2299.8 %reduce-scatter.22.cloned.1.call-start = ((), (), s32[]{:S(2)}) async-start(), calls=%async_computation.25 | async-start | bytes 21135360 | tf_op jit(solution)/shard_map/reduce_scatter | solution.py:341
  1556.4 9.1 collective-permute-start.24
  1557.7 9.1 collective-permute-start.25
  1561.6 15.2 collective-permute-start.26
  1562.9 15.2 collective-permute-start.27
  1564.2 16.0 collective-permute-start.28
  1565.5 16.6 collective-permute-start.29
  1566.8 17.9 collective-permute-start.30
  1576.8 15.7 collective-permute-start.31
  1578.1 26.2 collective-permute-start.32
  1580.2 28.3 collective-permute-start.33
  1582.2 32.2 collective-permute-start.34
  1584.7 31.9 collective-permute-start.35
  1592.5 26.1 collective-permute-start.36
  1604.3 16.8 collective-permute-start.37
  1608.5 15.4 collective-permute-start.38
  1614.4 10.9 collective-permute-start.39
  1616.6 9.9 collective-permute-start.40
  1618.6 9.3 collective-permute-start.41
  1621.2 10.2 collective-permute-start.42
  1624.0 10.0 collective-permute-start.43
  1625.3 10.3 collective-permute-start.44
  1626.6 12.0 collective-permute-start.10
  1627.9 13.2 collective-permute-start.11
  1631.3 11.3 collective-permute-start.12
  1633.9 11.0 collective-permute-start.13
  1635.6 11.2 collective-permute-start.14
  1638.6 11.4 collective-permute-start.15
  1641.1 11.1 collective-permute-start.16
  1642.6 12.8 collective-permute-start.17
  1645.0 11.8 collective-permute-start.18
  1646.8 11.3 collective-permute-start.19
  1650.1 12.1 collective-permute-start.2
  1652.3 11.2 collective-permute-start.20
  1655.4 10.0 collective-permute-start.21
  1656.7 12.0 collective-permute-start.22
  1658.1 13.0 collective-permute-start.3
  1662.2 12.9 collective-permute-start.4
  1663.5 44.8 %collective-permute-start.5 = (f32[24,160]{1,0:T(8,128)S(1)}, f32[24,160]{1,0:T(8,128)}, u32[]{:S(2)}, u32[]{:S(2)}) collective-permute-start(f32[24,160]{1,0:T(8,128)S(1)} %get-tuple-element.335), channel_id=1, source_target_pairs={{0,4},{1,5},{2,6},{3,7},{4,8},{5,9},{6,10},{7,11},{8,12},{9,13},{1... | collective-permute-start | bytes 46088
  1665.5 42.8 %collective-permute-start.6 = (f32[24,160]{1,0:T(8,128)S(1)}, f32[24,160]{1,0:T(8,128)}, u32[]{:S(2)}, u32[]{:S(2)}) collective-permute-start(f32[24,160]{1,0:T(8,128)S(1)} %get-tuple-element.335), channel_id=1, source_target_pairs={{0,5},{1,6},{2,7},{3,8},{4,9},{5,10},{6,11},{7,12},{8,13},{9,14},{... | collective-permute-start | bytes 46088
  1668.7 39.6 %collective-permute-start.7 = (f32[24,160]{1,0:T(8,128)S(1)}, f32[24,160]{1,0:T(8,128)}, u32[]{:S(2)}, u32[]{:S(2)}) collective-permute-start(f32[24,160]{1,0:T(8,128)S(1)} %get-tuple-element.335), channel_id=1, source_target_pairs={{0,6},{1,7},{2,8},{3,9},{4,10},{5,11},{6,12},{7,13},{8,14},{9,15},... | collective-permute-start | bytes 46088
  1671.0 37.3 %collective-permute-start.8 = (f32[24,160]{1,0:T(8,128)S(1)}, f32[24,160]{1,0:T(8,128)}, u32[]{:S(2)}, u32[]{:S(2)}) collective-permute-start(f32[24,160]{1,0:T(8,128)S(1)} %get-tuple-element.335), channel_id=1, source_target_pairs={{0,7},{1,8},{2,9},{3,10},{4,11},{5,12},{6,13},{7,14},{8,15},{9,16}... | collective-permute-start | bytes 46088
  1675.1 33.2 collective-permute-start.9
  1742.7 13.6 all-to-all-start.3
  1756.3 11.9 all-to-all-start.4
  1768.1 10.6 all-to-all-start.5
  (114 other events, 3152.4 us)
Sparse Core Ops, SparseCore 0:
  11.2 74.2 all-gather.14
  88.6 70.1 all-gather.16
  161.9 71.3 all-gather.18
  306.7 49.5 all-gather.22
  582.7 30.3 all-gather.20
  615.2 49.2 all-gather.24
  666.2 29.7 all-gather.28
  698.2 49.2 all-gather.26
  770.9 28.5 reduce-scatter.17
  801.9 29.3 reduce-scatter.15
  835.1 85.9 reduce-scatter.25
  1136.1 142.9 all-reduce.76
  1282.8 85.9 reduce-scatter.27
  1372.9 86.0 reduce-scatter.29
  1461.8 675.8 reduce-scatter.19
  2140.5 668.6 reduce-scatter.23
  2812.0 669.0 reduce-scatter.21
where the time goes:
time: 3520 us; the launch traced here: 3490 us
  waiting for transfers between devices  1840 us (52%)
  blocking collectives  730 us (21%)
  local copies, waits for them, and re-layouts  430 us (12%)
  other arithmetic  179 us (5%)
  matrix products  148 us (4%)
  starting transfers between devices  141 us (4%)
    reduce_scatter x1, waiting for transfers between devices, local(): lax.psum_scatter(grad_proj_x, ('seq', 'rows'), scatter_dimension=0, tiled...  672 us
    reduce_scatter x1, waiting for transfers between devices, local(): lax.psum_scatter(grad_proj_y, ('seq', 'rows'), scatter_dimension=0, tiled...  671 us
    unnamed x2, blocking collectives  430 us
    reduce_scatter x1, waiting for transfers between devices, local(): lax.psum_scatter(grad_proj_out, ('seq', 'rows'), scatter_dimension=0, til...  358 us
    unnamed x45, starting transfers between devices  121 us
    slice x41, local copies, waits for them, and re-layouts, local(): lax.associative_scan(combine, (next_factor, grad_states), reverse=True, a...  119 us
    unnamed x248, local copies, waits for them, and re-layouts  94.4 us
    all_gather x3, blocking collectives, prefix(): everything = jax.tree.map(lambda part: lax.all_gather(part, axis), value)  79.6 us
  transfers between devices with their start and end apart: 67, of which 10 were waited for; matrix products, arithmetic and copies ran while one was open for 31% of the time, Pallas kernels for 0%

commit v1 on v0

v1 whole, which is shorter than its diff:
```python
import jax
import jax.numpy as jnp
from jax import lax
from jax.experimental import pallas as pl
from jax.experimental.pallas import tpu as pltpu
from jax.sharding import PartitionSpec as P

BF, F32 = jnp.bfloat16, jnp.float32
MESH = pl.DeviceIdType.MESH
EPSILON = 1e-06
FLOOR_VALUE = 0.001
HID = 768
CH = 320
WIDE = 384
PK = 1024
FK = 2304
FG = 1536
TOK = 2176
SMALL = 32


def dot(left, right):
    return jnp.dot(left, right, preferred_element_type=F32)


def dot_last(left, right):
    return lax.dot_general(left, right, (((1,), (1,)), ((), ())), preferred_element_type=F32)


def dot_first(left, right):
    return lax.dot_general(left, right, (((0,), (0,)), ((), ())), preferred_element_type=F32)


def gelu(v):
    return 0.5 * v * (1.0 + jnp.tanh(0.7978845608028654 * (v + 0.044715 * (v * v * v))))


def gelu_and_slope(v):
    square = v * v
    t = jnp.tanh(0.7978845608028654 * v * (1.0 + 0.044715 * square))
    half = 0.5 * (1.0 + t)
    slope = half + 0.5 * v * (1.0 - t * t) * (0.7978845608028654 * (1.0 + 0.134145 * square))
    return v * half, slope


def turn(v, d):
    return lax.rem(v + (d % 4), 4)


class Place:
    def __init__(self):
        s, self.y = lax.axis_index("seq"), lax.axis_index("rows")
        self.x, self.z, self.c = lax.div(s, 8), lax.rem(lax.div(s, 2), 4), lax.rem(s, 2)
        self.plane = self.x * 4 + self.z
        self.part = self.y * 2 + self.c

    def at(self, x=None, z=None, c=None, y=None):
        x = self.x if x is None else x
        z = self.z if z is None else z
        c = self.c if c is None else c
        return (x * 8 + z * 2 + c, self.y if y is None else y)

    def sibling(self):
        return self.at(c=1 - self.c)

    def column(self, d):
        return turn(self.y, d // 2), (self.c + d % 2) % 2 if d % 2 == 0 else 1 - self.c

    def flat(self, d):
        p = lax.rem(self.plane + (d % 16), 16)
        return self.at(x=lax.div(p, 4), z=lax.rem(p, 4))


class Net:
    def __init__(self, send, recv, local):
        self.send, self.recv, self.near = send, recv, local
        self.names, self.sent, self.kept = {}, [], []

    def slot(self, name):
        assert len(self.names) < self.recv.shape[0] and len(self.sent) <= self.send.shape[0]
        return self.names.setdefault(name, len(self.names))

    def go(self, src, dst, to, name):
        copy = pltpu.make_async_remote_copy(
            src_ref=src,
            dst_ref=dst,
            send_sem=self.send.at[len(self.sent)],
            recv_sem=self.recv.at[self.slot(name)],
            device_id=to,
            device_id_type=MESH,
        )
        copy.start()
        self.sent.append(copy)
        return copy

    def many(self, copies, pieces):
        waits = []
        for src, dst, to, name in copies:
            waits.append(
                pltpu.make_async_remote_copy(
                    src_ref=src,
                    dst_ref=dst,
                    send_sem=self.send.at[len(self.sent)],
                    recv_sem=self.recv.at[self.slot(name)],
                    device_id=to,
                    device_id_type=MESH,
                )
            )
            self.sent.append(waits[-1])
        first = len(self.sent) - len(copies)
        for piece in range(pieces):
            for i, (src, dst, to, name) in enumerate(copies):
                rows = src.shape[-2] // pieces
                at = (slice(None),) * (len(src.shape) - 2) + (pl.ds(rows * piece, rows),)
                pltpu.make_async_remote_copy(
                    src_ref=src.at[at],
                    dst_ref=dst.at[at],
                    send_sem=self.send.at[first + i],
                    recv_sem=self.recv.at[self.slot(name)],
                    device_id=to,
                    device_id_type=MESH,
                ).start()
        return waits

    def take(self, dst, name, to):
        pltpu.make_async_remote_copy(
            src_ref=dst,
            dst_ref=dst,
            send_sem=self.send.at[0],
            recv_sem=self.recv.at[self.slot(name)],
            device_id=to,
            device_id_type=MESH,
        ).wait_recv()

    def local(self, src, dst):
        assert len(self.kept) < self.near.shape[0]
        copy = pltpu.make_async_copy(src, dst, self.near.at[len(self.kept)])
        copy.start()
        self.kept.append(copy)
        return copy

    def drain(self, but=()):
        for copy in self.sent:
            if all(copy is not other for other in but):
                copy.wait_send()


def greet(peers, extra=0):
    barrier = pltpu.get_barrier_semaphore()
    for peer in peers:
        pl.semaphore_signal(barrier, inc=1, device_id=peer, device_id_type=MESH)
    return barrier


def add_into(out, terms):
    rows = out.shape[-2]
    lead = [()]
    for extent in out.shape[:-2]:
        lead = [one + (i,) for one in lead for i in range(extent)]
    for one in lead:

        def step(i, _):
            at = pl.ds(pl.multiple_of(i * 16, 16), 16)
            if len(terms) == 2:
                total = terms[0][one + (at, slice(None))] + terms[1][one + (at, slice(None))]
            else:
                total = terms[0][one + (at, slice(None))].astype(F32)
                for term in terms[1:]:
                    total = total + term[one + (at, slice(None))].astype(F32)
            out[one + (at, slice(None))] = total.astype(out.dtype)
            return 0

        lax.fori_loop(0, rows // 16, step, 0, unroll=2)


class GatherColumn:
    def __init__(self, net, me, g, tag):
        self.net, self.me, self.g, self.tag = net, me, g, tag
        self.sent = []

    def go(self, *what):
        self.sent.append(self.net.go(*what))

    def block(self, dy, k, c):
        return self.g.at[2 * turn(self.me.y, dy) + k, c]

    def start(self, src):
        me, net, tag = self.me, self.net, self.tag
        copies = []
        for k in range(2):
            copies.append((src.at[k], self.block(0, k, me.c), me.at(y=turn(me.y, 1)), (tag, "ring", -1, k)))
            copies.append((src.at[1 - k], self.block(0, 1 - k, me.c), me.at(y=turn(me.y, -1)), (tag, "ring", 1, 1 - k)))
            copies.append((src.at[k], self.block(0, k, me.c), me.sibling(), (tag, "sib", 0, k)))
        for group in (copies[:3], copies[3:]):
            self.sent += net.many(group, 1)
        self.own = net.local(src, self.g.at[pl.ds(2 * me.y, 2), me.c])

    def relay(self, halves=(0, 1)):
        me, net, tag = self.me, self.net, self.tag
        for first in halves:
            copies = []
            for dy in (-1, 1):
                k = first if dy == -1 else 1 - first
                here = self.block(dy, k, me.c)
                net.take(here, (tag, "ring", dy, k), me.sibling())
                if first == 0:
                    copies.append((here, here, me.at(y=turn(me.y, -dy)), (tag, "far", k)))
                copies.append((here, here, me.sibling(), (tag, "sib", dy, k)))
            self.sent += net.many(copies, 1)

    def last(self):
        me, net, tag = self.me, self.net, self.tag
        for k in range(2):
            here = self.block(2, k, me.c)
            net.take(here, (tag, "far", k), me.sibling())
            self.go(here, here, me.sibling(), (tag, "sib", 2, k))

    def whole(self, dy):
        me, net, tag = self.me, self.net, self.tag
        if dy == 0:
            self.own.wait()
        for k in range(2):
            net.take(self.block(dy, k, 1 - me.c), (tag, "sib", dy, k), me.sibling())

    def finish(self):
        for dy in (0, -1, 1, 2):
            self.whole(dy)


class ReduceColumn:
    def __init__(self, net, me, part, pair, far, side, tag):
        self.net, self.me, self.tag = net, me, tag
        self.part, self.pair, self.far, self.side = part, pair, far, side
        self.sent = []

    def go(self, *what):
        self.sent.append(self.net.go(*what))

    def drain(self):
        for copy in self.sent:
            copy.wait_send()

    def mine(self, dy):
        return self.part.at[pl.ds(2 * turn(self.me.y, dy), 2), self.me.c]

    def one(self, dy, k):
        return self.part.at[2 * turn(self.me.y, dy) + k, self.me.c]

    def send_pair(self, dy):
        me = self.me
        src = self.part.at[pl.ds(2 * turn(me.y, dy), 2), 1 - me.c]
        self.go(src, self.pair.at[dy % 4], me.sibling(), (self.tag, "pair", dy % 4))

    def take_pair(self, dy):
        me, net, tag = self.me, self.net, self.tag
        net.take(self.pair.at[dy % 4], (tag, "pair", dy % 4), me.sibling())
        add_into(self.mine(dy), (self.mine(dy), self.pair.at[dy % 4]))
        above, below = me.at(y=turn(me.y, 1)), me.at(y=turn(me.y, -1))
        if dy == 2:
            self.go(self.one(2, 0), self.far.at[0], above, (tag, "far", 0))
            self.go(self.one(2, 1), self.far.at[1], below, (tag, "far", 1))
        elif dy == 1:
            self.go(self.one(1, 1), self.side.at[0, 1], above, (tag, "side", 0, 1))
        elif dy == -1:
            self.go(self.one(-1, 0), self.side.at[1, 0], below, (tag, "side", 1, 0))

    def relay(self):
        me, net, tag = self.me, self.net, self.tag
        above, below = me.at(y=turn(me.y, 1)), me.at(y=turn(me.y, -1))
        net.take(self.far.at[0], (tag, "far", 0), below)
        add_into(self.one(1, 0), (self.one(1, 0), self.far.at[0]))
        self.go(self.one(1, 0), self.side.at[0, 0], above, (tag, "side", 0, 0))
        net.take(self.far.at[1], (tag, "far", 1), above)
        add_into(self.one(-1, 1), (self.one(-1, 1), self.far.at[1]))
        self.go(self.one(-1, 1), self.side.at[1, 1], below, (tag, "side", 1, 1))

    def arrive(self):
        for way in range(2):
            for k in range(2):
                self.net.take(self.side.at[way, k], (self.tag, "side", way, k), self.me.sibling())

    def total(self, k, at):
        return (
            self.one(0, k)[at, :].astype(F32)
            + self.side[0, k, at, :].astype(F32)
            + self.side[1, k, at, :].astype(F32)
        )


class GatherPlane:
    def __init__(self, net, me, g, tag, pieces):
        self.net, self.me, self.g, self.tag, self.pieces = net, me, g, tag, pieces
        self.sent = []

    def block(self, h, da, db):
        me = self.me
        if h == 0:
            return self.g.at[turn(me.x, db), turn(me.z, da), 0]
        return self.g.at[turn(me.x, da), turn(me.z, db), 1]

    def peer(self, h, da, db):
        me = self.me
        if h == 0:
            return me.at(x=turn(me.x, db), z=turn(me.z, da))
        return me.at(x=turn(me.x, da), z=turn(me.z, db))

    def copy(self, h, da, db, step_a, step_b, rows=None):
        here = self.block(h, da, db)
        name = (self.tag, h, (da - step_a) % 4, (db - step_b) % 4)
        if rows is not None:
            here = here.at[pl.ds(32 * rows, 32)]
            name += (rows,)
        return (here, here, self.peer(h, step_a, step_b), name)

    def send(self, copies):
        self.sent += self.net.many([self.copy(*one) for one in copies], self.pieces)

    def take(self, h, da, db, rows=None):
        here = self.block(h, da, db)
        name = (self.tag, h, da % 4, db % 4)
        if rows is not None:
            here = here.at[pl.ds(32 * rows, 32)]
            name += (rows,)
        self.net.take(here, name, self.me.sibling())

    def start(self):
        self.send([(h, 0, 0, step, 0) for h in range(2) for step in (1, -1)])
        self.send([(h, 0, 0, 0, step) for h in range(2) for step in (1, -1)])

    def second(self):
        for h in range(2):
            self.take(h, -1, 0)
            self.take(h, 1, 0)
        self.send(
            [(h, -step, 0, step, 0, 0 if step == 1 else 1) for h in range(2) for step in (1, -1)]
        )
        for da in (-1, 1):
            self.send([(h, da, 0, 0, step) for h in range(2) for step in (1, -1)])

    def third(self):
        for h in range(2):
            self.take(h, 0, -1)
            self.take(h, 0, 1)
        self.send([(h, 0, -1, 0, 1) for h in range(2)])
        for h in range(2):
            self.take(h, 2, 0, rows=0)
            self.take(h, 2, 0, rows=1)
        self.send([(h, 2, 0, 0, step) for h in range(2) for step in (1, -1)])

    def fourth(self):
        for h in range(2):
            self.take(h, -1, -1)
            self.take(h, -1, 1)
            self.take(h, 1, -1)
            self.take(h, 1, 1)
        self.send([(h, da, 1, 0, -1) for da in (-1, 1) for h in range(2)])

    def fifth(self):
        for h in range(2):
            self.take(h, 2, -1)
            self.take(h, 2, 1)
        self.send([(h, 2, -1, 0, 1) for h in range(2)])

    def finish(self):
        for h in range(2):
            for da in (0, -1, 1, 2):
                self.take(h, da, 2)


class ReducePlane:
    def __init__(self, net, me, g, far, side, far2, side2, tag):
        self.net, self.me, self.g, self.tag = net, me, g, tag
        self.far, self.side, self.far2, self.side2 = far, side, far2, side2

    def super(self, h, db, lo, g=None):
        me = self.me
        g = self.g if g is None else g
        if h == 0:
            return g.at[turn(me.x, db), pl.ds(lo, 2), 0]
        return g.at[pl.ds(lo, 2), turn(me.z, db), 1]

    def whole(self, h, a):
        me = self.me
        return self.g.at[me.x, a, 0] if h == 0 else self.g.at[a, me.z, 1]

    def along(self, h, db):
        me = self.me
        return me.at(x=turn(me.x, db)) if h == 0 else me.at(z=turn(me.z, db))

    def across(self, h, da):
        me = self.me
        return me.at(z=turn(me.z, da)) if h == 0 else me.at(x=turn(me.x, da))

    def start(self, g=None):
        net, tag = self.net, self.tag
        far, side = [], []
        for h in range(2):
            far.append((self.super(h, 2, 0, g), self.far.at[h, 0], self.along(h, 1), (tag, h, "far", 0)))
            far.append((self.super(h, 2, 2, g), self.far.at[h, 1], self.along(h, -1), (tag, h, "far", 1)))
            to = self.side.at[h, 0, pl.ds(2, 2)]
            side.append((self.super(h, 1, 2, g), to, self.along(h, 1), (tag, h, "side", 0, 1)))
            to = self.side.at[h, 1, pl.ds(0, 2)]
            side.append((self.super(h, -1, 0, g), to, self.along(h, -1), (tag, h, "side", 1, 0)))
        net.many(far, 1)
        net.many(side, 1)

    def second(self):
        net, tag = self.net, self.tag
        for h in range(2):
            for way in range(2):
                here = self.far.at[h, way]
                net.take(here, (tag, h, "far", way), self.me.sibling())
                step = 1 if way == 0 else -1
                add_into(here, (here, self.super(h, step, 2 * way)))
                net.go(
                    here, self.side.at[h, way, pl.ds(2 * way, 2)], self.along(h, step), (tag, h, "side", way, way)
                )

    def third(self):
        net, tag = self.net, self.tag
        for h in range(2):
            for way in range(2):
                for lo in range(2):
                    here = self.side.at[h, way, pl.ds(2 * lo, 2)]
                    net.take(here, (tag, h, "side", way, lo), self.me.sibling())
        me = self.me
        for h in range(2):
            mine = me.z if h == 0 else me.x
            for da in (2, 1, -1, 0):
                a = turn(mine, da)
                here = self.side.at[h, 0, a]
                add_into(here, (here, self.side.at[h, 1, a], self.whole(h, a)))
                if da == 2:
                    for way in range(2):
                        net.go(
                            here.at[pl.ds(32 * way, 32)],
                            self.far2.at[h, way],
                            self.across(h, 1 if way == 0 else -1),
                            (tag, h, "far2", way),
                        )
                elif da != 0:
                    way = 0 if da == 1 else 1
                    rows = pl.ds(32 * (1 - way), 32)
                    net.go(
                        here.at[rows], self.side2.at[h, way, rows], self.across(h, da), (tag, h, "side2", way, 1 - way)
                    )

    def fourth(self):
        net, tag, me = self.net, self.tag, self.me
        for h in range(2):
            mine = me.z if h == 0 else me.x
            for way in range(2):
                here = self.far2.at[h, way]
                net.take(here, (tag, h, "far2", way), me.sibling())
                da = 1 if way == 0 else -1
                rows = pl.ds(32 * way, 32)
                add_into(here, (here, self.side.at[h, 0, turn(mine, da), rows]))
                net.go(here, self.side2.at[h, way, rows], self.across(h, da), (tag, h, "side2", way, way))

    def finish(self):
        net, tag, me = self.net, self.tag, self.me
        for h in range(2):
            mine = me.z if h == 0 else me.x
            for way in range(2):
                for part in range(2):
                    here = self.side2.at[h, way, pl.ds(32 * part, 32)]
                    net.take(here, (tag, h, "side2", way, part), me.sibling())
            here = self.side2.at[h, 0]
            add_into(here, (here, self.side2.at[h, 1], self.side.at[h, 0, mine]))


def column_peers(me):
    peers = []
    for d in range(1, 8):
        y, c = me.column(d)
        peers.append(me.at(y=y, c=c))
    return peers


def one_less_exp(t, plain):
    series = 1.0 - t * (1.0 / 8.0)
    for k in range(7, 1, -1):
        series = 1.0 - t * (1.0 / k) * series
    return jnp.where(t < 0.5, t * series, plain)


def decay_parts(rate, log_scale, resets):
    log_decay = rate * log_scale
    a = jnp.exp(log_decay)
    margin = one_less_exp(-2.0 * log_decay, 1.0 - a * a)
    scale = jnp.where(resets > 0.5, 1.0, jnp.sqrt(jnp.maximum(margin, FLOOR_VALUE)))
    return a, a * (1.0 - resets), scale, margin


def log_scale_row(vec):
    return -8.0 * jax.nn.softplus(-vec[7:8, :])


STEP = 32


def blocks(first, count, body):
    def one(i, _):
        row, j = first + lax.div(i, 128 // STEP), lax.rem(i, 128 // STEP)
        at = pl.ds(pl.multiple_of(j * STEP, STEP), STEP)
        body(row, j, at)
        return 0

    lax.fori_loop(0, count * (128 // STEP), one, 0, unroll=2)


def mask_block(masks, row, j):
    inner = 64 // STEP
    at = pl.ds(pl.multiple_of(lax.rem(j, inner) * STEP, STEP), STEP)
    return masks[row, lax.div(j, inner), at, :].astype(F32)


def lanes_below(shape, limit):
    return lax.broadcasted_iota(jnp.int32, shape, len(shape) - 1) < limit


def forward_kernel(
    px, py, po, wg, wu, wd, tokens_in, cot_in, seg, rate_in, input_in, odds_in,
    p_out, one_out, mask_out, gain_out, vec_out, riw_out, ce_out,
    pre_out, co_out, rt_out, ig_out, st_out, carry_out, mix_out, gf_out, gd_out, gb_out, pout_out, res_out, gres_out, gain2_out,
    pxl, pyl, pol, wp, rate_l, input_l, odds, sm, x1, gt, gpart,
    pbuf, wf, xg, sg, small, riw, vec, gains, ce, pre, co, rt, ig, fa, st, mix, car, carry, pair, far, side, res, two, xo,
    s2, ct, cot, hid, gu, pout, gb, gres, gain2, flip, far_d, side_d, far2_d, side2_d,
    send, recv, local, ssend, srecv,
):
    me = Place()
    net = Net(send, recv, local)
    loads = [
        net.local(a, b)
        for a, b in (
            (px, pxl), (py, pyl), (po, pol), (odds_in, odds), (rate_in, rate_l), (input_in, input_l), (tokens_in, xo), (cot_in, cot)
        )
    ]
    to_y, to_c, index = me.x, lax.div(me.z, 2), lax.rem(me.z, 2) * 8 + me.c * 4 + me.y
    mine = jnp.logical_and(to_y == me.y, to_c == me.c)

    def small_from(j):
        return me.at(x=me.y, z=2 * me.c + j // 8, c=(j // 4) % 2, y=j % 4)

    def small_to(p):
        return me.at(x=p // 4, z=p % 4, c=to_c, y=to_y)

    barrier = greet(column_peers(me) + [me.flat(d) for d in range(1, 16)])
    for i in range(16):

        @pl.when(jnp.logical_not(jnp.logical_and(mine, me.plane == i)))
        def _():
            pl.semaphore_signal(barrier, inc=1, device_id=small_to(i), device_id_type=MESH)

        @pl.when(jnp.logical_not(jnp.logical_and(mine, index == i)))
        def _():
            pl.semaphore_signal(barrier, inc=1, device_id=small_from(i), device_id_type=MESH)

    spot = lax.broadcasted_iota(jnp.int32, (64, 128), 0) + (me.plane * 2 + me.c) * 64
    lane = lax.broadcasted_iota(jnp.int32, (64, 128), 1)
    for k in range(2):
        reset, crossed = jnp.zeros((64, 128), F32), jnp.zeros((64, 128), F32)
        for j in range(4):
            start = seg[k, j]
            reset = jnp.where(spot == start, 1.0, reset)
            crossed = jnp.where(jnp.logical_and(start <= spot, start > spot - lane), 1.0, crossed)
        usable = jnp.where(jnp.logical_and(lane <= 3, spot >= lane), 1.0 - crossed, 0.0)
        x1[k, :, 2048:TOK] = jnp.where(lane == 0, reset, usable).astype(BF)

    for copy in loads[:6]:
        copy.wait()
    zeros = jnp.zeros((16, 256), F32)
    for t in range(8):
        low, shift = 128 * (CH * t // 128), CH * t % 128

        def window(ref):
            wide = ref[:, low : low + WIDE].astype(F32)
            wide = pltpu.roll(wide, WIDE - shift, 1) if shift else wide
            return jnp.where(lanes_below((16, WIDE), CH), wide, 0.0)

        both = jnp.concatenate([window(pxl), zeros], axis=1)
        both = both + pltpu.roll(jnp.concatenate([window(pyl), zeros], axis=1), CH, 1)
        wp[t, :, 0:640] = both.astype(BF)
        wp[t, :, 640:PK] = window(pol).astype(BF)
    small[0:32, :] = jnp.zeros((32, WIDE), F32)
    small[0:20, 0:160] = rate_l[...].astype(F32)
    left = small[0:32, :]
    small[0:20, 0:160] = input_l[...].astype(F32)
    left = left + pltpu.roll(small[0:32, :], 160, 1)
    small[0:32, :] = left
    small[24:32, 0:128] = odds[0:8, :]
    sm[...] = small[0:32, :].astype(BF)
    gt[...] = pltpu.roll(odds[8:16, :], me.c * 64 + me.y * 16, 1)
    pl.semaphore_wait(barrier, 22 + 32 - 2 * mine.astype(jnp.int32))

    def p_block(y, c):
        return pbuf.at[me.x, me.z, c, pl.ds(pl.multiple_of(16 * y, 16), 16)]

    def f_block(y, c, k):
        rows = pl.ds(pl.multiple_of(16 * y, 16), 16)
        return wf.at[me.x, me.z, c, rows, pl.ds(HID * k, HID)]

    def features(p):
        return pl.ds(pl.multiple_of(128 * p, 128), 128)

    for d in range(1, 8):
        y, c = me.column(d)
        net.go(gt, gpart.at[d], me.at(y=y, c=c), ("gain8", d))
    for d in range(1, 8):
        y, c = me.column(d)
        net.go(wp.at[2 * y + c], p_block(me.y, me.c), me.at(y=y, c=c), ("wp", d))
    own_p = net.local(wp.at[me.part], p_block(me.y, me.c))
    total = gt[...]
    for d in range(1, 8):
        net.take(gpart.at[d], ("gain8", d), me.sibling())
        total = total + gpart[d]
    gpart[0] = total
    gains[:, features(me.plane)] = total
    for d in range(1, 16):
        net.go(gpart.at[0], gains.at[:, features(me.plane)], me.flat(d), ("gain", d))

    def source(d):
        return turn(me.y, -(d // 2)), me.c if d % 2 == 0 else 1 - me.c

    for d in range(1, 8):
        net.take(p_block(*source(d)), ("wp", d), me.sibling())
    own_p.wait()
    proj = GatherPlane(net, me, pbuf, "p", 1)
    proj.start()
    loads[6].wait()
    for d in range(1, 16):
        net.take(gains.at[:, features(lax.rem(me.plane + 16 - d, 16))], ("gain", d), me.sibling())
    for k in range(2):

        def norm_step(i, _):
            at = pl.ds(pl.multiple_of(i * 16, 16), 16)
            x = xo[k, at, :].astype(F32)
            scale = lax.rsqrt(jnp.mean(x * x, axis=-1, keepdims=True) + EPSILON)
            x1[k, at, 0:2048] = (x * scale * gains[0:1, :]).astype(BF)
            return 0

        lax.fori_loop(0, 4, norm_step, 0, unroll=2)
    tokens = GatherColumn(net, me, xg, "x")
    tokens.start(x1)
    proj.second()

    def small_copy(i):
        return pltpu.make_async_remote_copy(
            src_ref=sm,
            dst_ref=sg.at[index],
            send_sem=ssend.at[i],
            recv_sem=srecv.at[index],
            device_id=small_to(i),
            device_id_type=MESH,
        )

    for i in range(16):
        own = jnp.logical_and(mine, me.plane == i)

        @pl.when(jnp.logical_not(own))
        def _():
            small_copy(i).start()

        @pl.when(own)
        def _():
            pltpu.make_async_copy(sm, sg.at[index], srecv.at[index]).start()

    tokens.relay((0,))
    proj.third()
    for d in range(1, 8):
        y, c = me.column(d)
        for k, w in enumerate((wg, wu, wd)):
            cols = pl.ds(pl.multiple_of(HID * (2 * y + c), HID), HID)
            net.go(w.at[:, cols], f_block(me.y, me.c, k), me.at(y=y, c=c), ("wf", d, k))
    own_f = []
    for k, w in enumerate((wg, wu, wd)):
        cols = pl.ds(pl.multiple_of(HID * me.part, HID), HID)
        own_f.append(net.local(w.at[:, cols], f_block(me.y, me.c, k)))
    proj.fourth()
    tokens.relay((1,))
    proj.fifth()
    tokens.last()

    small[...] = jnp.zeros_like(small)
    for j in range(16):

        @pl.when(jnp.logical_not(jnp.logical_and(mine, index == j)))
        def _():
            pltpu.make_async_remote_copy(
                src_ref=sm,
                dst_ref=sg.at[j],
                send_sem=ssend.at[0],
                recv_sem=srecv.at[j],
                device_id=me.sibling(),
                device_id_type=MESH,
            ).wait_recv()

        @pl.when(jnp.logical_and(mine, index == j))
        def _():
            pltpu.make_async_copy(sm, sg.at[j], srecv.at[j]).wait()

    vectors = jnp.zeros((8, WIDE), F32)
    inside = lanes_below((8, WIDE), 20)
    for j in range(16):
        block = sg[j].astype(F32)
        small[20 * j : 20 * j + 20, :] = block[0:20, :]
        vectors = vectors + pltpu.roll(jnp.where(inside, block[24:32, :], 0.0), 20 * j, 1)
    vec[...] = vectors
    rows = lax.broadcasted_iota(jnp.int32, (WIDE, WIDE), 0)
    lanes = lax.broadcasted_iota(jnp.int32, (WIDE, WIDE), 1)
    held = small[...]
    first = jnp.logical_and(rows < 160, lanes < 160)
    second = jnp.logical_and(jnp.logical_and(rows >= 160, rows < CH), jnp.logical_and(lanes >= 160, lanes < CH))
    riw[:, 0:WIDE] = (jnp.where(first, held, 0.0) + jnp.where(second, pltpu.roll(held, 160, 1), 0.0)).astype(BF)
    riw[:, WIDE:] = (
        jnp.where(first, pltpu.roll(held, WIDE - 160, 1), 0.0) + jnp.where(second, held, 0.0)
    ).astype(BF)
    for d in range(1, 8):
        for k in range(3):
            net.take(f_block(*source(d), k), ("wf", d, k), me.sibling())
    for copy in own_f:
        copy.wait()
    feed = GatherPlane(net, me, wf, "f", 1)
    feed.start()
    loads[7].wait()
    cots = GatherColumn(net, me, ct, "c")
    cots.start(cot)
    proj.finish()
    tokens.finish()
    masks = xg.at[:, :, :, pl.ds(2048, 128)]

    def project(i, _):
        at = pl.ds(2 * i, 2)
        left = xg[at, :, :, 0:2048].reshape(256, 2048)
        both = dot(left, pbuf[:, :, :, :, 0:640].reshape(2048, 640))
        low = jnp.where(lanes_below((256, WIDE), CH), both[:, 0:WIDE], 0.0).astype(BF)
        ce[at, 16:144, :] = low.reshape(2, 128, WIDE)
        right = jnp.where(lanes_below((256, WIDE), CH), pltpu.roll(both[:, 256:640], WIDE - 64, 1), 0.0)
        pre[at] = right.reshape(2, 128, WIDE)
        return 0

    lax.fori_loop(0, 4, project, 0)
    for copy in tokens.sent:
        copy.wait_send()
    wide = xg.at[:, :, :, pl.ds(0, 2048)]
    save_one = net.local(wide, one_out)
    net.go(ce.at[:, pl.ds(128, 16)], ce.at[:, pl.ds(0, 16)], me.flat(1), "halo")
    cots.relay()
    net.take(ce.at[:, pl.ds(0, 16)], "halo", me.sibling())

    def convolve(row, j, at):
        wide = ce[row, pl.ds(pl.multiple_of(j * STEP, STEP), STEP + 16), :].astype(F32)
        valid = mask_block(masks, row, j)
        total = jnp.broadcast_to(vec[4:5, :], (STEP, WIDE))
        for k in range(4):
            piece = wide[16 - k : 16 - k + STEP, :]
            if k > 0:
                piece = piece * valid[:, k : k + 1]
            total = total + vec[k : k + 1, :] * piece
        co[row, at, :] = total

    blocks(0, 8, convolve)
    feed.second()

    def gates(i, _):
        at = pl.ds(4 * i, 4)
        both = dot(co[at].reshape(512, WIDE).astype(BF), riw[...])
        rt[at] = both[:, 0:WIDE].reshape(4, 128, WIDE)
        ig[at] = both[:, WIDE:].reshape(4, 128, WIDE)
        return 0

    lax.fori_loop(0, 2, gates, 0)
    log_scale = log_scale_row(vec)

    def decays(row, j, at):
        rate = jax.nn.sigmoid(rt[row, at, :] + vec[5:6, :])
        gate = jax.nn.sigmoid(ig[row, at, :] + vec[6:7, :])
        _, factor, scale, _ = decay_parts(rate, log_scale, mask_block(masks, row, j)[:, 0:1])
        rt[row, at, :] = rate
        ig[row, at, :] = gate
        fa[row, at, :] = factor
        st[row, at, :] = scale * (gate * co[row, at, :])

    blocks(0, 8, decays)
    cots.last()
    feed.third()

    def scan(i, held):
        h, q = held
        at = pl.ds(pl.multiple_of(i * 8, 8), 8)
        f, d = jnp.swapaxes(fa[:, at, :], 0, 1), jnp.swapaxes(st[:, at, :], 0, 1)
        hs, qs = [], []
        for k in range(8):
            h, q = f[k] * h + d[k], q * f[k]
            hs.append(h)
            qs.append(q)
        st[:, at, :] = jnp.swapaxes(jnp.stack(hs), 0, 1)
        fa[:, at, :] = jnp.swapaxes(jnp.stack(qs), 0, 1)
        return h, q

    h, q = lax.fori_loop(0, 16, scan, (jnp.zeros((8, WIDE), F32), jnp.ones((8, WIDE), F32)), unroll=2)
    car[me.plane, 0] = q
    car[me.plane, 1] = h
    for d in range(1, 16):
        net.go(car.at[me.plane], car.at[me.plane], me.flat(d), ("carry", d))
    for d in range(1, 16):
        net.take(car.at[lax.rem(me.plane + 16 - d, 16)], ("carry", d), me.sibling())
    h = jnp.zeros((8, WIDE), F32)
    for k in range(15):
        h = jnp.where(k < me.plane, car[k, 0] * h + car[k, 1], h)
    carry[...] = h
    branch = ReduceColumn(net, me, wide, pair, far, side, "branch")
    save_one.wait()
    feed.fourth()

    def outward(dy):
        first = 2 * turn(me.y, dy)

        def mixing(row, j, at):
            states = st[row, at, :] + fa[row, at, :] * carry[pl.ds(row, 1), :]
            st[row, at, :] = states
            mix[row, at, :] = (states * gelu(pre[row, at, :])).astype(BF)

        blocks(first, 2, mixing)
        at = pl.ds(first, 2)

        def onto(n, _):
            low = dot_last(mix[at].reshape(256, WIDE), pbuf[n, :, :, :, 640:1024].reshape(512, WIDE)).astype(BF)
            xg[at, :, :, pl.ds(pl.multiple_of(512 * n, 512), 512)] = low.reshape(2, 2, 64, 512)
            return 0

        lax.fori_loop(0, 4, onto, 0)
        branch.send_pair(dy)

    outward(2)
    outward(1)
    branch.take_pair(2)
    outward(-1)
    branch.take_pair(1)
    outward(0)
    branch.take_pair(-1)
    feed.fifth()
    keep = [
        net.local(src, dst)
        for src, dst in (
            (rt, rt_out), (ig, ig_out), (co, co_out), (pbuf, p_out), (masks, mask_out), (gains, gain_out),
            (vec, vec_out), (riw, riw_out), (ce, ce_out), (pre, pre_out), (st, st_out), (carry, carry_out),
            (mix, mix_out),
        )
    ]
    branch.relay()
    branch.take_pair(0)
    branch.arrive()
    for k in range(2):

        def close_branch(i, _):
            at = pl.ds(pl.multiple_of(i * 16, 16), 16)
            value = xo[k, at, :].astype(F32) + branch.total(k, at)
            res[k, at, :] = value
            scale = lax.rsqrt(jnp.mean(value * value, axis=-1, keepdims=True) + EPSILON)
            two[k, at, :] = (value * scale * gains[1:2, :]).astype(BF)
            return 0

        lax.fori_loop(0, 4, close_branch, 0, unroll=2)
    branch.drain()
    scaled = GatherColumn(net, me, s2, "two")
    scaled.start(two)
    cots.finish()
    for copy in keep[:3]:
        copy.wait()
    feed.finish()

    def ahead(*dys):
        count = 2 * len(dys)
        first = [turn(me.y, dy) for dy in dys]
        for ref, source, k in ((rt, s2, 0), (ig, s2, 1), (co, ct, 2)):
            left = jnp.concatenate([source[pl.ds(2 * yy, 2)].reshape(256, 2048) for yy in first], axis=0)
            product = dot(left, wf[:, :, :, :, HID * k : HID * (k + 1)].reshape(2048, HID))
            ref[0:count] = product[:, 0:WIDE].reshape(count, 128, WIDE)
            ref[count : 2 * count] = product[:, WIDE:].reshape(count, 128, WIDE)
        for number, yy in enumerate(first):

            def bend(j, _):
                row = lax.div(j, 8)
                here = pl.ds(pl.multiple_of(16 * lax.rem(j, 8), 16), 16)
                rows = pl.ds(pl.multiple_of(256 * yy + 16 * j, 16), 16)
                for half in range(2):
                    lanes = slice(WIDE * half, WIDE * (half + 1))
                    at = count * half + 2 * number + row
                    up, grad = ig[at, here, :], co[at, here, :]
                    act, slant = gelu_and_slope(rt[at, here, :])
                    hid[rows, lanes] = (act * up).astype(BF)
                    gu[rows, lanes] = (grad * (up * slant)).astype(BF)
                    gu[rows, HID + WIDE * half : HID + WIDE * (half + 1)] = (grad * act).astype(BF)
                return 0

            lax.fori_loop(0, 16, bend, 0)

    scaled.whole(0)
    ahead(0)
    scaled.relay()
    scaled.whole(1)
    scaled.whole(-1)
    ahead(1, -1)
    scaled.last()
    scaled.whole(2)
    ahead(2)
    slope = ReduceColumn(net, me, wide, pair, far, side, "slope")

    def inner(*dys):
        first = [turn(me.y, dy) for dy in dys]

        def out(n, _):
            left = [gu[pl.ds(pl.multiple_of(256 * yy, 256), 256), :] for yy in first]
            low = dot_last(jnp.concatenate(left, axis=0), wf[n, :, :, :, 0:FG].reshape(512, FG)).astype(BF)
            at = pl.ds(pl.multiple_of(512 * n, 512), 512)
            for number, yy in enumerate(first):
                xg[pl.ds(2 * yy, 2), :, :, at] = low[256 * number : 256 * (number + 1)].reshape(2, 2, 64, 512)
            return 0

        lax.fori_loop(0, 4, out, 0)
        for dy in dys:
            slope.send_pair(dy)

    def down(n, _):
        low = dot_last(hid[...], wf[n, :, :, :, FG:].reshape(512, HID)).astype(BF)
        pout[:, :, :, pl.ds(pl.multiple_of(512 * n, 512), 512)] = low.reshape(8, 2, 64, 512)
        return 0

    inner(2, 1)
    slope.take_pair(2)
    slope.take_pair(1)
    inner(-1, 0)
    slope.take_pair(-1)
    slope.relay()
    slope.take_pair(0)
    lax.fori_loop(0, 4, down, 0)

    def store(i):
        lanes = pl.ds(0, FG)
        return pltpu.make_async_copy(wf.at[i, :, :, :, lanes], gf_out.at[i], ssend.at[i])

    def columns(i):
        return pl.ds(pl.multiple_of(512 * i, 512), 512)

    def weights_down(i, _):
        flip[...] = jnp.transpose(ct[:, :, :, columns(i)].reshape(1024, 512))
        wf[i, :, :, :, FG:] = dot(flip[...], hid[...]).astype(BF).reshape(4, 2, 64, HID)
        return 0

    def weights(i, _):
        flip[...] = jnp.transpose(s2[:, :, :, columns(i)].reshape(1024, 512))
        for k in range(2):
            lanes = slice(HID * k, HID * (k + 1))
            wf[i, :, :, :, lanes] = dot(flip[...], gu[:, lanes]).astype(BF).reshape(4, 2, 64, HID)
        store(i).start()
        return 0

    under = ReducePlane(net, me, wf.at[:, :, :, :, pl.ds(FG, HID)], far_d, side_d, far2_d, side2_d, "d")

    for i in range(16):

        @pl.when(jnp.logical_not(jnp.logical_and(mine, me.plane == i)))
        def _():
            small_copy(i).wait_send()

    gain2[...] = jnp.zeros_like(gain2)
    for copy in feed.sent:
        copy.wait_send()
    lax.fori_loop(0, 4, weights_down, 0)
    under.start()
    slope.arrive()
    for k in range(2):

        def close(i, _):
            at = pl.ds(pl.multiple_of(i * 16, 16), 16)
            value = res[k, at, :]
            scale = lax.rsqrt(jnp.mean(value * value, axis=-1, keepdims=True) + EPSILON)
            normed = value * scale
            got = slope.total(k, at)
            gain2[0:8, :] = gain2[0:8, :] + (got * normed).reshape(2, 8, 2048).sum(axis=0)
            v = got * gains[1:2, :]
            back = (v - normed * jnp.mean(v * normed, axis=-1, keepdims=True)) * scale
            total = cot[k, at, :].astype(F32) + back
            gres[k, at, :] = total
            gb[k, at, :] = total.astype(BF)
            return 0

        lax.fori_loop(0, 4, close, 0, unroll=2)
    back = GatherColumn(net, me, gb_out, "gb")
    back.start(gb)
    keep += [net.local(gres, gres_out), net.local(gain2, gain2_out), net.local(pout, pout_out), net.local(res, res_out)]
    under.second()
    lax.fori_loop(0, 2, weights, 0)
    back.relay((0,))
    under.third()
    lax.fori_loop(2, 3, weights, 0)
    back.relay((1,))
    lax.fori_loop(3, 4, weights, 0)
    back.last()
    under.fourth()
    under.finish()
    keep.append(net.local(side2_d.at[:, 0], gd_out))
    for i in range(4):
        store(i).wait()
    back.finish()
    for copy in keep[3:]:
        copy.wait()
    net.drain(tokens.sent + branch.sent + feed.sent)


def backward_kernel(
    gb_in, p_in, gf_in, one_in, mask_in, gain_in, vec_in, riw_in, ce_in, pre_in, co_in, rt_in, ig_in, st_in, mix_in,
    carry_in, gres_in, gain2_in, x_in, pout_in, res_in, gd_in,
    ff_out, fd_out, fo_out, fi_out, small_out, gains_out, gx_out, out_out,
    gb, w, gf, masks, gains, vec, riw, ce, pre, co, rt, ig, st, mix, carry, gres, gain2, xo,
    gm, fa, car, edge, z, sgr, srec, ssum, part, pair, far, side, pair2, far2, side2, res, out, gpi, far_f, side_f, far2_f, side2_f,
    far_o, side_o, far2_o, side2_o, far_i, side_i, far2_i, side2_i, ff, fd, fo, fi, grow, gsum, gtot, gall, gx, wacc, halo,
    send, recv, local, ssend, srecv,
):
    me = Place()
    net = Net(send, recv, local)
    loads = {
        name: net.local(a, b)
        for name, a, b in (
            ("gb", gb_in, gb), ("w", p_in, w), ("pre", pre_in, pre), ("st", st_in, st), ("part", pout_in, part), ("mix", mix_in, mix),
            ("rt", rt_in, rt), ("masks", mask_in, masks), ("vec", vec_in, vec), ("gf", gf_in, gf), ("co", co_in, co),
            ("ig", ig_in, ig), ("carry", carry_in, carry), ("riw", riw_in, riw), ("ce", ce_in, ce),
            ("gains", gain_in, gains), ("gres", gres_in, gres), ("gain2", gain2_in, gain2), ("x", x_in, xo), ("res", res_in, res),
        )
    }

    def need(*names):
        for name in names:
            loads[name].wait()

    to_y, to_c, index = me.x, lax.div(me.z, 2), lax.rem(me.z, 2) * 8 + me.c * 4 + me.y
    mine = jnp.logical_and(to_y == me.y, to_c == me.c)

    def small_to(j):
        return me.at(x=me.y, z=2 * me.c + j // 8, c=(j // 4) % 2, y=j % 4)

    def small_from(p):
        return me.at(x=p // 4, z=p % 4, c=to_c, y=to_y)

    barrier = greet(column_peers(me) + [me.flat(d) for d in range(1, 16)])
    for i in range(16):

        @pl.when(jnp.logical_not(jnp.logical_and(mine, me.plane == i)))
        def _():
            pl.semaphore_signal(barrier, inc=1, device_id=small_from(i), device_id_type=MESH)

        @pl.when(jnp.logical_not(jnp.logical_and(mine, index == i)))
        def _():
            pl.semaphore_signal(barrier, inc=1, device_id=small_to(i), device_id_type=MESH)

    pl.semaphore_wait(barrier, 22 + 32 - 2 * mine.astype(jnp.int32))
    feed = ReducePlane(net, me, gf, far_f, side_f, far2_f, side2_f, "f")
    result = ReduceColumn(net, me, part, pair2, far2, side2, "result")
    gpo = w.at[:, :, :, :, pl.ds(640, WIDE)]
    outer = ReducePlane(net, me, gpo, far_o, side_o, far2_o, side2_o, "o")
    inner = ReducePlane(net, me, gpi, far_i, side_i, far2_i, side2_i, "i")
    feed.start(gf_in)

    def share(source, dst, tag):
        for d in range(1, 8):
            y, c = me.column(d)
            src = source.at[c, pl.ds(pl.multiple_of(16 * y, 16), 16)]
            net.go(src, dst.at[me.part], me.at(y=y, c=c), (tag, d))
        src = source.at[me.c, pl.ds(pl.multiple_of(16 * me.y, 16), 16)]
        return net.local(src, dst.at[me.part])

    def collect(dst, tag):
        for d in range(1, 8):
            y = turn(me.y, -(d // 2))
            c = me.c if d % 2 == 0 else 1 - me.c
            net.take(dst.at[2 * y + c], (tag, d), me.sibling())

    own_d = share(gd_in, fd, "fd")
    need("gb", "w")

    def mix_back(i, _):
        at = pl.ds(4 * i, 4)
        grad = dot(gb[at].reshape(512, 2048), w[:, :, :, :, 640:1024].reshape(2048, WIDE))
        gm[at] = grad.reshape(4, 128, WIDE)
        return 0

    lax.fori_loop(0, 2, mix_back, 0)
    need("part")
    for dy in (2, 1, -1, 0):
        result.send_pair(dy)
    need("pre", "st", "rt", "masks", "vec")
    log_scale = log_scale_row(vec)

    def bend_back(row, j, at):
        act, slant = gelu_and_slope(pre[row, at, :])
        grad = jnp.where(lanes_below((STEP, WIDE), CH), gm[row, at, :], 0.0)
        low = grad * st[row, at, :] * slant
        z[row, at, 256:640] = pltpu.roll(low, 64, 1).astype(BF)
        gm[row, at, :] = grad * act
        _, factor, _, _ = decay_parts(rt[row, at, :], log_scale, mask_block(masks, row, j)[:, 0:1])
        fa[row, at, :] = factor

    blocks(0, 8, bend_back)

    def scan(step, held):
        g, m = held
        at = pl.ds(pl.multiple_of((15 - step) * 8, 8), 8)
        f, d = jnp.swapaxes(fa[:, at, :], 0, 1), jnp.swapaxes(gm[:, at, :], 0, 1)
        las, lps = [None] * 8, [None] * 8
        for k in range(7, -1, -1):
            la = d[k] + g
            las[k], lps[k] = la, m
            g, m = f[k] * la, f[k] * m
        gm[:, at, :] = jnp.swapaxes(jnp.stack(las), 0, 1)
        fa[:, at, :] = jnp.swapaxes(jnp.stack(lps), 0, 1)
        return g, m

    g, m = lax.fori_loop(0, 16, scan, (jnp.zeros((8, WIDE), F32), jnp.ones((8, WIDE), F32)), unroll=2)
    car[me.plane, 0] = m
    car[me.plane, 1] = g
    for d in range(1, 16):
        net.go(car.at[me.plane], car.at[me.plane], me.flat(d), ("carry", d))
    need("mix", "gf")

    def weight_out(i, _):
        left = gb[:, :, :, pl.ds(pl.multiple_of(512 * i, 512), 512)].reshape(1024, 512)
        w[i, :, :, :, 640:1024] = dot_first(left, mix[...].reshape(1024, WIDE)).astype(BF).reshape(4, 2, 64, WIDE)
        return 0

    lax.fori_loop(0, 4, weight_out, 0)
    load_one = net.local(one_in, gb)
    feed.second()
    outer.start()
    for dy in (2, 1, -1, 0):
        result.take_pair(dy)
    for d in range(1, 16):
        net.take(car.at[lax.rem(me.plane + 16 - d, 16)], ("carry", d), me.sibling())
    g = jnp.zeros((8, WIDE), F32)
    for k in range(15, 0, -1):
        g = jnp.where(k > me.plane, car[k, 1] + car[k, 0] * g, g)
    edge[...] = g
    wacc[...] = jnp.zeros_like(wacc)
    need("co", "ig", "carry", "riw", "ce")

    def fold(value):
        return value.reshape(STEP // 8, 8, WIDE).sum(axis=0)

    def gate_back(row, j, at):
        resets = mask_block(masks, row, j)[:, 0:1]
        adjoint = gm[row, at, :] + fa[row, at, :] * edge[pl.ds(row, 1), :]
        rate, gate, conv = rt[row, at, :], ig[row, at, :], co[row, at, :]
        a, factor, scale, margin = decay_parts(rate, log_scale, resets)
        before = st[row, pl.ds(pl.multiple_of(jnp.maximum(j * STEP - 8, 0), 8), 8), :]
        edge_row = jnp.where(j == 0, carry[pl.ds(row, 1), :], before[7:8, :])
        top = lax.broadcasted_iota(jnp.int32, (STEP, WIDE), 0) == 0
        previous = jnp.where(top, edge_row, pltpu.roll(st[row, at, :], 1, 0))
        grad_scale = adjoint * gate * conv
        free = jnp.logical_and(margin > FLOOR_VALUE, resets < 0.5)
        grad_log = adjoint * previous * factor - jnp.where(free, grad_scale * (a * a) / scale, 0.0)
        rate_pre = grad_log * log_scale * rate * (1.0 - rate)
        through = adjoint * scale
        gate_pre = through * conv * gate * (1.0 - gate)
        wacc[5] = wacc[5] + fold(rate_pre)
        wacc[6] = wacc[6] + fold(gate_pre)
        wacc[7] = wacc[7] + fold(grad_log * rate)
        gm[row, at, :] = through * gate
        rt[row, at, :] = rate_pre
        ig[row, at, :] = gate_pre

    blocks(0, 8, gate_back)
    result.relay()

    def through_gates(i, _):
        at = pl.ds(4 * i, 4)
        total = gm[at].reshape(512, WIDE)
        total = total + dot_last(rt[at].reshape(512, WIDE).astype(BF), riw[:, 0:WIDE])
        total = total + dot_last(ig[at].reshape(512, WIDE).astype(BF), riw[:, WIDE:])
        gm[at] = total.reshape(4, 128, WIDE)
        return 0

    lax.fori_loop(0, 2, through_gates, 0)

    def conv_back(row, j, at):
        wide = ce[row, pl.ds(pl.multiple_of(j * STEP, STEP), STEP + 16), :].astype(F32)
        valid = mask_block(masks, row, j)
        grad = gm[row, at, :]
        wacc[4] = wacc[4] + fold(grad)
        total = jnp.zeros((STEP + 8, WIDE), F32)
        for k in range(4):
            kept = grad if k == 0 else grad * valid[:, k : k + 1]
            wacc[k] = wacc[k] + fold(kept * wide[16 - k : 16 - k + STEP, :])
            scaled = kept * vec[k : k + 1, :]
            total = total + jnp.concatenate(
                [jnp.zeros((8 - k, WIDE), F32), scaled] + ([jnp.zeros((k, WIDE), F32)] if k else []), axis=0
            )
        fa[row, at, :] = total[8:, :]
        early = total[0:8, :]

        @pl.when(j == 0)
        def _():
            halo[0, row] = early

        @pl.when(j > 0)
        def _():
            last = pl.ds(pl.multiple_of(j * STEP - 8, 8), 8)
            fa[row, last, :] = fa[row, last, :] + early

    blocks(0, 8, conv_back)
    net.go(halo.at[0], halo.at[1], me.flat(-1), "halo")
    feed.third()
    outer.second()

    net.take(halo.at[1], "halo", me.sibling())

    def conv_in_back(row, j, at):
        grad = fa[row, at, :]
        tail = jnp.where(j == 128 // STEP - 1, halo[1, row], 0.0)
        grad = grad + jnp.concatenate([jnp.zeros((STEP - 8, WIDE), F32), tail], axis=0)
        z[row, at, 0:256] = grad[:, 0:256].astype(BF)
        late = jnp.where(lanes_below((STEP, 128), 64), grad[:, 256:384], z[row, at, 256:384].astype(F32))
        z[row, at, 256:384] = late.astype(BF)

    blocks(0, 8, conv_in_back)
    result.arrive()
    result.drain()
    need("res")
    for k in range(2):

        def close_result(i, _):
            at = pl.ds(pl.multiple_of(i * 16, 16), 16)
            out[k, at, :] = (res[k, at, :] + result.total(k, at)).astype(BF)
            return 0

        lax.fori_loop(0, 4, close_result, 0, unroll=2)
    save_out = net.local(out, out_out)
    entry = ReduceColumn(net, me, part, pair, far, side, "entry")

    def inward(dy):
        at = pl.ds(2 * turn(me.y, dy), 2)

        def out(n, _):
            low = dot_last(z[at].reshape(256, 640), w[n, :, :, :, 0:640].reshape(512, 640)).astype(BF)
            part[at, :, :, pl.ds(pl.multiple_of(512 * n, 512), 512)] = low.reshape(2, 2, 64, 512)
            return 0

        lax.fori_loop(0, 4, out, 0)
        entry.send_pair(dy)

    def weight_in(i, _):
        left = gb[:, :, :, pl.ds(pl.multiple_of(512 * i, 512), 512)].reshape(1024, 512)
        gpi[i] = dot_first(left, z[...].reshape(1024, 640)).astype(BF).reshape(4, 2, 64, 640)
        return 0

    load_one.wait()
    lax.fori_loop(0, 4, weight_in, 0)
    inner.start()
    inward(2)
    inward(1)
    entry.take_pair(2)
    inner.second()
    inward(-1)
    entry.take_pair(1)
    inward(0)
    entry.take_pair(-1)
    feed.fourth()
    inner.third()
    entry.relay()
    entry.take_pair(0)
    outer.third()
    feed.finish()
    own_f = share(side2_f.at[:, 0], ff, "ff")
    inner.fourth()
    outer.fourth()
    low = co[...].reshape(1024, WIDE).astype(BF)
    grad_rate = dot_first(low, rt[...].reshape(1024, WIDE).astype(BF))
    grad_gate = dot_first(low, ig[...].reshape(1024, WIDE).astype(BF))
    rows = lax.broadcasted_iota(jnp.int32, (WIDE, WIDE), 0)
    lanes = lax.broadcasted_iota(jnp.int32, (WIDE, WIDE), 1)
    upper = rows < 160
    held = jnp.where(
        lanes < 160,
        jnp.where(upper, grad_rate, pltpu.roll(grad_rate, WIDE - 160, 1)),
        jnp.where(upper, pltpu.roll(grad_gate, 160, 1), grad_gate),
    )
    vectors = jnp.concatenate([jnp.sum(wacc[k], axis=0, keepdims=True) for k in range(8)], axis=0)
    slope = -8.0 * -jax.nn.sigmoid(-vec[7:8, :])
    line = lax.broadcasted_iota(jnp.int32, (8, WIDE), 0)
    vectors = jnp.where(line == 7, vectors * slope, vectors)
    tall = jnp.transpose(jnp.concatenate([vectors, jnp.zeros((120, WIDE), F32)], axis=0))
    gm[0:3] = held.reshape(3, 128, WIDE)
    late = jnp.where(lanes_below((WIDE, 128), 64), held[:, 256:384], pltpu.roll(tall, 64, 1))
    gm[0:3, :, 256:384] = late.reshape(3, 128, 128)
    flat = gm[0:3].reshape(WIDE, WIDE)
    for j in range(16):
        piece = jnp.concatenate([flat[20 * j : 20 * j + 20, :], jnp.zeros((12, WIDE), F32)], axis=0)
        sgr[j] = piece.astype(BF)

    def small_copy(j):
        return pltpu.make_async_remote_copy(
            src_ref=sgr.at[j],
            dst_ref=srec.at[me.plane],
            send_sem=ssend.at[j],
            recv_sem=srecv.at[me.plane],
            device_id=small_to(j),
            device_id_type=MESH,
        )

    for j in range(16):
        own = jnp.logical_and(mine, index == j)

        @pl.when(jnp.logical_not(own))
        def _():
            small_copy(j).start()

        @pl.when(own)
        def _():
            pltpu.make_async_copy(sgr.at[j], srec.at[me.plane], srecv.at[me.plane]).start()

    need("gains", "gres", "gain2", "x")
    grow[...] = jnp.zeros_like(grow)
    entry.arrive()
    for k in range(2):

        def close(i, _):
            at = pl.ds(pl.multiple_of(i * 16, 16), 16)
            value = xo[k, at, :].astype(F32)
            scale = lax.rsqrt(jnp.mean(value * value, axis=-1, keepdims=True) + EPSILON)
            normed = value * scale
            got = entry.total(k, at)
            grow[...] = grow[...] + (got * normed).reshape(2, 8, 2048).sum(axis=0)
            v = got * gains[0:1, :]
            back = (v - normed * jnp.mean(v * normed, axis=-1, keepdims=True)) * scale
            gx[k, at, :] = (gres[k, at, :] + back).astype(BF)
            return 0

        lax.fori_loop(0, 4, close, 0, unroll=2)
    keep = [net.local(gx, gx_out), save_out]
    line = lax.broadcasted_iota(jnp.int32, (8, 2048), 0)
    one = jnp.broadcast_to(jnp.sum(grow[...], axis=0, keepdims=True), (8, 2048))
    two = jnp.broadcast_to(jnp.sum(gain2[...], axis=0, keepdims=True), (8, 2048))
    grow[...] = jnp.where(line == 0, one, jnp.where(line == 1, two, 0.0))

    def features(p):
        return pl.ds(pl.multiple_of(128 * p, 128), 128)

    for d in range(1, 16):
        p = lax.rem(me.plane + d, 16)
        net.go(grow.at[:, features(p)], gsum.at[me.plane], me.flat(d), ("gain", d))
    gsum[me.plane] = grow[:, features(me.plane)]

    inner.finish()
    own_i = share(side2_i.at[:, 0], fi, "fi")
    outer.finish()
    own_o = share(side2_o.at[:, 0], fo, "fo")
    for p in range(16):

        @pl.when(jnp.logical_not(jnp.logical_and(mine, me.plane == p)))
        def _():
            pltpu.make_async_remote_copy(
                src_ref=sgr.at[0],
                dst_ref=srec.at[p],
                send_sem=ssend.at[0],
                recv_sem=srecv.at[p],
                device_id=me.sibling(),
                device_id_type=MESH,
            ).wait_recv()

        @pl.when(jnp.logical_and(mine, me.plane == p))
        def _():
            pltpu.make_async_copy(sgr.at[0], srec.at[p], srecv.at[p]).wait()

    total = srec[0].astype(F32)
    for k in range(1, 16):
        total = total + srec[k].astype(F32)
    ssum[...] = total
    keep.append(net.local(ssum, small_out))
    for d in range(1, 16):
        net.take(gsum.at[lax.rem(me.plane + 16 - d, 16)], ("gain", d), me.sibling())
    total = gsum[0]
    for k in range(1, 16):
        total = total + gsum[k]
    gall[me.part] = total
    for d in range(1, 8):
        y, c = me.column(d)
        net.go(gall.at[me.part], gall.at[me.part], me.at(y=y, c=c), ("gain8", d))
    own_f.wait()
    collect(ff, "ff")
    keep.append(net.local(ff, ff_out))
    own_d.wait()
    collect(fd, "fd")
    keep.append(net.local(fd, fd_out))
    collect(gall, "gain8")
    total = gall[0]
    for k in range(1, 8):
        total = total + gall[k]
    gtot[...] = total
    keep.append(net.local(gtot, gains_out))
    own_o.wait()
    collect(fo, "fo")
    keep.append(net.local(fo, fo_out))
    own_i.wait()
    collect(fi, "fi")
    keep.append(net.local(fi, fi_out))
    for copy in keep:
        copy.wait()
    net.drain(result.sent)
    for j in range(16):

        @pl.when(jnp.logical_not(jnp.logical_and(mine, index == j)))
        def _():
            small_copy(j).wait_send()


def shaped(shape, kind):
    return jax.ShapeDtypeStruct(shape, kind)


def vmem(shape, kind):
    return pltpu.VMEM(shape, kind)


def call(kernel, args, outs, scratch, name, number, sends, recvs, extra=(), places={}):
    anywhere = pl.BlockSpec(memory_space=pl.ANY)
    return pl.pallas_call(
        kernel,
        out_shape=[shaped(*out) for out in outs],
        in_specs=[places.get(i, anywhere) for i in range(len(args))],
        out_specs=[anywhere] * len(outs),
        scratch_shapes=[vmem(*one) for one in scratch]
        + [pltpu.SemaphoreType.DMA((sends,)), pltpu.SemaphoreType.DMA((recvs,)), pltpu.SemaphoreType.DMA((48,))]
        + list(extra),
        compiler_params=pltpu.CompilerParams(
            collective_id=number, has_side_effects=True, vmem_limit_bytes=62 * 1024 * 1024
        ),
        name=name,
    )(*args)


ROWS = (8, 128, WIDE)
BLOCK = (2, 64, 2048)
ALL = (8, 2, 64, 2048)
SIXTEEN = (pltpu.SemaphoreType.DMA((16,)), pltpu.SemaphoreType.DMA((16,)))


def plane(width):
    return [((2, 2, 2, 64, width), BF), ((2, 2, 4, 64, width), BF), ((2, 2, 32, width), BF), ((2, 2, 64, width), BF)]


def forward(args):
    weights = (4, 4, 2, 64)
    flat = pl.BlockSpec(memory_space=pltpu.SMEM)
    sums = [((4,) + BLOCK, BF), (BLOCK, BF), ((2,) + BLOCK, BF)]
    return call(
        forward_kernel,
        args,
        [
            (weights + (PK,), BF), (ALL, BF), ((8, 2, 64, 128), BF), ((8, 2048), F32), ((8, WIDE), F32),
            ((WIDE, 2 * WIDE), BF), ((8, 144, WIDE), BF),
            (ROWS, F32), (ROWS, F32), (ROWS, F32), (ROWS, F32), (ROWS, F32), ((8, WIDE), F32), (ROWS, BF),
            (weights + (FG,), BF), ((2, 64, HID), BF), (ALL, BF), (ALL, BF), (BLOCK, F32), (BLOCK, F32),
            ((8, 2048), F32),
        ],
        [
            ((16, 2560), BF), ((16, 2560), BF), ((16, 2560), BF), ((8, 16, PK), BF), ((20, 160), BF), ((20, 160), BF),
            ((16, 128), F32), ((SMALL, WIDE), BF), ((2, 64, TOK), BF), ((8, 128), F32), ((8, 8, 128), F32),
            (weights + (PK,), BF), (weights + (FK,), BF), ((8, 2, 64, TOK), BF), ((16, SMALL, WIDE), BF),
            ((WIDE, WIDE), F32), ((WIDE, 2 * WIDE), BF), ((8, WIDE), F32), ((8, 2048), F32), ((8, 144, WIDE), BF),
            (ROWS, F32), (ROWS, F32), (ROWS, F32), (ROWS, F32), (ROWS, F32), (ROWS, F32), (ROWS, BF),
            ((16, 2, 8, WIDE), F32), ((8, WIDE), F32), *sums, (BLOCK, F32), (BLOCK, BF), (BLOCK, BF),
            (ALL, BF), (ALL, BF), (BLOCK, BF), ((1024, HID), BF), ((1024, FG), BF),
            (ALL, BF), (BLOCK, BF), (BLOCK, F32), ((8, 2048), F32), ((512, 1024), BF), *plane(HID),
        ],
        "forward", 1, 256, 256, SIXTEEN, {8: flat},
    )


def backward(args):
    return call(
        backward_kernel,
        args,
        [
            ((8, 16, FG), BF), ((8, 16, HID), BF), ((8, 16, WIDE), BF), ((8, 16, 640), BF), ((SMALL, WIDE), F32), ((8, 128), F32),
            (BLOCK, BF), (BLOCK, BF),
        ],
        [
            (ALL, BF), ((4, 4, 2, 64, PK), BF), ((4, 4, 2, 64, FG), BF), ((8, 2, 64, 128), BF), ((8, 2048), F32),
            ((8, WIDE), F32), ((WIDE, 2 * WIDE), BF), ((8, 144, WIDE), BF), (ROWS, F32), (ROWS, F32), (ROWS, F32),
            (ROWS, F32), (ROWS, F32), (ROWS, BF), ((8, WIDE), F32), (BLOCK, F32), ((8, 2048), F32), (BLOCK, BF),
            (ROWS, F32), (ROWS, F32), ((16, 2, 8, WIDE), F32), ((8, WIDE), F32), ((8, 128, 640), BF),
            ((16, SMALL, WIDE), BF), ((16, SMALL, WIDE), BF), ((SMALL, WIDE), F32),
            (ALL, BF), ((4,) + BLOCK, BF), (BLOCK, BF), ((2,) + BLOCK, BF),
            ((4,) + BLOCK, BF), (BLOCK, BF), ((2,) + BLOCK, BF), (BLOCK, F32), (BLOCK, BF), ((4, 4, 2, 64, 640), BF),
            *plane(FG), *plane(WIDE), *plane(640),
            ((8, 16, FG), BF), ((8, 16, HID), BF), ((8, 16, WIDE), BF), ((8, 16, 640), BF),
            ((8, 2048), F32), ((16, 8, 128), F32), ((8, 128), F32),
            ((8, 8, 128), F32), (BLOCK, BF), ((8, 8, WIDE), F32), ((2, 8, 8, WIDE), F32),
        ],
        "recurrent_backward", 3, 256, 256, SIXTEEN,
    )


def finish_kernel(
    ff_in, fd_in, fo_in, fi_in, small_in, sums_in, gx_in, result_in,
    output, grad_tokens, gain_a, gain_b, conv_w, conv_b, rate_w, input_w, rate_b, input_b, decay,
    out_w, x_w, y_w, gate_w, up_w, down_w,
    ff, fd, fo, fi, small, sums, sems,
):
    me = Place()
    moves = (
        (ff_in, ff), (fd_in, fd), (fo_in, fo), (fi_in, fi), (small_in, small), (sums_in, sums), (gx_in, grad_tokens),
        (result_in, output),
    )
    loads = [pltpu.make_async_copy(a, b, sems.at[i]) for i, (a, b) in enumerate(moves)]
    for copy in loads:
        copy.start()
    for copy in loads:
        copy.wait()
    own = pltpu.roll(sums[...], 128 - (me.c * 64 + me.y * 16), 1)
    gain_a[...] = own[0:1, 0:16]
    gain_b[...] = own[1:2, 0:16]
    rate_w[...] = small[0:20, 0:160]
    input_w[...] = pltpu.roll(small[0:20, :], WIDE - 160, 1)[:, 0:160]
    tall = jnp.concatenate([small[:, 256:384], jnp.zeros((128 - SMALL, 128), F32)], axis=0)
    vectors = jnp.transpose(tall)[64:72, 0:20]
    conv_w[...] = vectors[0:4, :]
    conv_b[...] = vectors[4:5, :]
    rate_b[...] = vectors[5:6, :]
    input_b[...] = vectors[6:7, :]
    decay[...] = vectors[7:8, :]
    for t in range(8):
        at = slice(HID * t, HID * (t + 1))
        gate_w[:, at] = ff[t, :, 0:HID].astype(F32)
        up_w[:, at] = ff[t, :, HID:].astype(F32)
        down_w[:, at] = fd[t].astype(F32)
    zeros = jnp.zeros((16, 256), F32)

    def pair(first, second):
        keep = lanes_below((16, WIDE), CH)
        left = jnp.concatenate([jnp.where(keep, first, 0.0), zeros], axis=1)
        right = jnp.concatenate([jnp.where(keep, second, 0.0), zeros], axis=1)
        return left + pltpu.roll(right, CH, 1)

    for t in range(0, 8, 2):
        at = slice(CH * t, CH * (t + 2))
        out_w[:, at] = pair(fo[t].astype(F32), fo[t + 1].astype(F32))
        x_w[:, at] = pair(fi[t, :, 0:WIDE].astype(F32), fi[t + 1, :, 0:WIDE].astype(F32))
        late = [pltpu.roll(fi[t + i, :, 256:640].astype(F32), WIDE - 64, 1) for i in range(2)]
        y_w[:, at] = pair(*late)


def finish(args):
    held = pl.BlockSpec(memory_space=pltpu.VMEM)
    outs = [
        (BLOCK, BF), (BLOCK, BF), ((1, 16), F32), ((1, 16), F32), ((4, 20), F32), ((1, 20), F32), ((20, 160), F32),
        ((20, 160), F32), ((1, 20), F32), ((1, 20), F32), ((1, 20), F32), ((16, 2560), F32), ((16, 2560), F32),
        ((16, 2560), F32), ((16, 6144), F32), ((16, 6144), F32), ((16, 6144), F32),
    ]
    return pl.pallas_call(
        finish_kernel,
        out_shape=[shaped(*out) for out in outs],
        in_specs=[pl.BlockSpec(memory_space=pl.ANY)] * len(args),
        out_specs=[held] * len(outs),
        scratch_shapes=[
            vmem((8, 16, FG), BF), vmem((8, 16, HID), BF), vmem((8, 16, WIDE), BF), vmem((8, 16, 640), BF),
            vmem((SMALL, WIDE), F32), vmem((8, 128), F32), pltpu.SemaphoreType.DMA((8,)),
        ],
        compiler_params=pltpu.CompilerParams(vmem_limit_bytes=62 * 1024 * 1024),
        name="results",
    )(*args)


def local(
    tokens,
    seg_starts,
    gain_one,
    gain_two,
    conv_weight,
    conv_bias,
    rate_weight,
    input_weight,
    rate_bias,
    input_bias,
    decay_param,
    proj_out,
    proj_x,
    proj_y,
    ffn_gate,
    ffn_up,
    ffn_down,
    cotangent,
):
    vectors = jnp.concatenate([conv_weight, jnp.stack([conv_bias, rate_bias, input_bias, decay_param])], axis=0)
    odds = jnp.concatenate(
        [
            jnp.pad(vectors, ((0, 0), (0, 108))),
            jnp.pad(jnp.stack([gain_one, gain_two]), ((0, 6), (0, 112))),
        ],
        axis=0,
    ).astype(F32)
    (
        p_all, one, mask_all, gains, vec, riw, ce, pre, co, rt, ig, st, carry, mix, gf, gd, gb, pout, res, gres, gain2
    ) = forward((
        proj_x, proj_y, proj_out, ffn_gate, ffn_up, ffn_down, tokens, cotangent, seg_starts, rate_weight, input_weight,
        odds,
    ))
    ff, fd, fo, fi, small, gain_sums, grad_tokens, output = backward((
        gb, p_all, gf, one, mask_all, gains, vec, riw, ce, pre, co, rt, ig, st, mix, carry, gres, gain2, tokens, pout, res,
        gd,
    ))
    results = finish((ff, fd, fo, fi, small, gain_sums, grad_tokens, output))
    return tuple(one.reshape(one.shape[1:]) if i in (2, 3, 5, 8, 9, 10) else one for i, one in enumerate(results))


def solution(mesh):
    both = ("seq", "rows")
    wide, flat = P(both, None), P(both)
    rows = P("rows", "seq", None)
    return jax.shard_map(
        local,
        mesh=mesh,
        in_specs=(
            rows, P("rows", None), flat, flat, P(None, both), flat, wide, wide, flat, flat, flat,
            wide, wide, wide, wide, wide, wide, rows,
        ),
        out_specs=(
            rows, rows, flat, flat, P(None, both), flat, wide, wide, flat, flat, flat,
            wide, wide, wide, wide, wide, wide,
        ),
        check_vma=False,
    )
```

time: 3520 us -> 322 us (0.09)
  waiting for transfers between devices: 1840 us -> 0 us
  blocking collectives: 730 us -> 0 us
  local copies, waits for them, and re-layouts: 430 us -> 0.74 us
  Pallas kernels: 0 us -> 318 us
  other arithmetic: 179 us -> 1.29 us
  matrix products: 148 us -> 0 us
  starting transfers between devices: 141 us -> 0 us
    reduce_scatter x8 -> x0, waiting for transfers between devices: 1700 us -> none  [the longest x1 672 us: local(): lax.psum_scatter(grad_proj_x, ('seq', 'rows'), scatter_dimension=0, tiled...]
    unnamed x2 -> x0, blocking collectives: 430 us -> none
    pallas_call x0 -> x3, Pallas kernels: none -> 318 us  [the longest x2 315 us: call(): pl.pallas_call(kernel, out_shape=[shaped(*out) for out in outs], in_specs...]
    all_gather x6 -> x0, blocking collectives: 279 us -> none  [the longest x3 79.6 us: prefix(): everything = jax.tree.map(lambda part: lax.all_gather(part, axis), value)]
    slice x81 -> x0, local copies, waits for them, and re-layouts: 182 us -> none  [the longest x41 119 us: local(): lax.associative_scan(combine, (next_factor, grad_states), reverse=True, a...]
    dot_general x24 -> x0, matrix products: 148 us -> none  [the longest x6 50.6 us: contract_first(): lax.dot_general(left, right, (((0,), (0,)), ((), ())), preferred_element_...]
    all_gather x8 -> x0, waiting for transfers between devices: 123 us -> none  [the longest x1 51.5 us: local(): lax.all_gather(down_cols, 'seq', axis=0, tiled=True)]
    unnamed x45 -> x0, starting transfers between devices: 121 us -> none
  transfers between devices with their start and end apart: 67 -> 0, of which waited for: 10 -> 0; matrix products, arithmetic and copies ran while one was open for 31% -> 0% of each run, Pallas kernels for 0% -> 0%
where the time goes in v1:
time: 322 us; the launch traced here: 321 us
  Pallas kernels  318 us (99%)
    pallas_call x2, Pallas kernels, call(): pl.pallas_call(kernel, out_shape=[shaped(*out) for out in outs], in_specs...  315 us

profile of v1, /device:TPU:0, one launch (start us, length us, event | category | flops | bytes accessed | tf_op | source)
XLA Modules:
  0.0 320.7 jit_solution(1082234676088118816)
XLA Ops:
  0.7 0.7 fusion.8
  1.3 0.7 concatenate.6
  2.1 0.6 fusion.2.odds_in
  2.7 211.5 %forward.1 = (bf16[4,4,2,64,1024]{4,3,2,1,0:T(8,128)(2,1)}, bf16[8,2,64,2048]{3,2,1,0:T(8,128)(2,1)}, bf16[8,2,64,128]{3,2,1,0:T(8,128)(2,1)}, f32[8,2048]{1,0:T...) custom-call(bf16[16,2560]{1,0:T(8,128)(2,1)} %px.1, ...), custom_call_target="tpu_custom_call" | custom-call | tf_op jit(solution)/shard_map/forward/pallas_call | solution.py:1425
  214.2 103.1 %recurrent_backward.1 = (bf16[8,16,1536]{2,1,0:T(8,128)(2,1)}, bf16[8,16,768]{2,1,0:T(8,128)(2,1)}, bf16[8,16,384]{2,1,0:T(8,128)(2,1)}, bf16[8,16,640]{2,1,0:T(...) custom-call(bf16[8,2,64,2048]{3,2,1,0:T(8,128)(2,1)} %get-tuple-elem, ...), custom_call_target="tpu_custom_call" | custom-call | tf_op jit(solution)/shard_map/recurrent_backward/pallas_call | solution.py:1425
  317.3 3.2 results.1
